TPU v7x, 32 devices: a whole 2x2x4 slice. The times are simulated.
32 devices in a mesh: section: 4 (over z), dp: 8 (over y, x, core).
Axes of the slice: x: 2, y: 2, z: 4, core: 2. Of those that a mesh axis runs over, the one named last changes fastest.
Arguments:
- block_input: bfloat16 [16, 512, 768], P('dp'), may hold values from -6 to 6
- out_cotangent: bfloat16 [16, 512, 768], P('dp'), may hold values from -6 to 6
- lengths: int32 [16], P('dp'), may hold values from 128 to 512, as said below
- ln_gain: float32 [4, 768], P('section'), may hold values from 0.5 to 1.5
- ln_bias: float32 [4, 768], P('section'), may hold values from -0.5 to 0.5
- w_in: bfloat16 [4, 768, 1536], P('section'), may hold values from -0.21875 to 0.21875
- b_in: bfloat16 [4, 1536], P('section'), may hold values from -3 to 3
- w_out: bfloat16 [4, 1536, 768], P('section'), may hold values from -0.109375 to 0.109375
- b_out: bfloat16 [4, 384], P('section'), may hold values from -3 to 3
Outputs:
- section_outputs: bfloat16 [4, 16, 512, 768], P('section', 'dp')
- input_grads: float32 [4, 16, 512, 768], P('section', 'dp')
- ln_gain_grad: float32 [4, 768], P('section')
- ln_bias_grad: float32 [4, 768], P('section')
- w_in_grad: float32 [4, 768, 1536], P('section')
- b_in_grad: float32 [4, 1536], P('section')
- w_out_grad: float32 [4, 1536, 768], P('section')
- b_out_grad: float32 [4, 384], P('section')
Inputs may be any that keep to these rules, and one draw needn't show every extreme that they name: `lengths`: each row uses at least a quarter of its slots, and in every draw some row uses all 512.
All inputs are finite; a program needn't handle non-finite values.
Results may differ from a plain program's by a relative error of at most 0.015.
Values may be sent and summed in bfloat16 or wider, within the bound.
A program may use at most 128 MiB of HBM per device.

v0:
```python
import math

import jax
import jax.numpy as jnp
from jax import lax
from jax.sharding import PartitionSpec as P

EPS = 1e-05


def passed_along(block, axis, distance):
    devices = range(lax.axis_size(axis))
    route = [(i - distance, i) for i in devices if i - distance in devices]
    return lax.ppermute(block, axis, route)


def as_sent(x):
    return jax.tree.map(lambda a: a.astype(jnp.bfloat16) if a.dtype == jnp.float32 else a, x)


def dft_pair(length):
    positions = jnp.arange(length, dtype=jnp.int32)
    turns = positions[:, None] * positions[None, :] % length
    angle = turns.astype(jnp.float32) * (2.0 * math.pi / length)
    scale = 1.0 / math.sqrt(length)
    return (jnp.cos(angle) * scale, jnp.sin(angle) * scale)


def exact_gelu(values):
    return jax.nn.gelu(values, approximate=False)


def normalize(summed):
    centre = summed - jnp.mean(summed, axis=-1, keepdims=True)
    spread = jnp.mean(centre * centre, axis=-1, keepdims=True)
    inverse = lax.rsqrt(spread + EPS)
    return (centre * inverse, inverse)


def norm_backward(upstream, mask_col, normed, inverse, norm_gain):
    masked = upstream * mask_col
    gain_term = jnp.sum(masked * normed, axis=0)
    bias_term = jnp.sum(masked, axis=0)
    scaled = masked * norm_gain
    inner = (
        scaled
        - jnp.mean(scaled, axis=-1, keepdims=True)
        - normed * jnp.mean(scaled * normed, axis=-1, keepdims=True)
    )
    return (inverse * inner, gain_term, bias_term)


def contract_rows(left, right):
    return lax.dot_general(
        left, right, (((0,), (0,)), ((), ())), preferred_element_type=jnp.float32
    )


def contract_cols(left, right):
    return lax.dot_general(
        left, right, (((1,), (1,)), ((), ())), preferred_element_type=jnp.float32
    )


def per_device(block_input, out_cotangent, lengths, ln_gain, ln_bias, w_in, b_in, w_out, b_out):
    micro_count = block_input.shape[0]
    seq_len = block_input.shape[1]
    width = block_input.shape[2]
    half_hidden = w_in.shape[2]
    half_width = b_out.shape[1]
    section_index = lax.axis_index("section")
    parity = section_index % 2
    last_section = lax.axis_size("section") - 1
    tick_count = micro_count + last_section
    partner = passed_along((w_in, b_in, w_out, b_out), "section", 1)
    w_first = jnp.concatenate([partner[0][0], w_in[0]], axis=1)
    bias_first = jnp.concatenate([partner[1][0], b_in[0]]).astype(jnp.float32)
    w_second = jnp.concatenate([partner[2][0], w_out[0]], axis=0)
    bias_second = jnp.concatenate([partner[3][0], b_out[0]]).astype(jnp.float32)
    norm_gain = ln_gain[0]
    norm_bias = ln_bias[0]
    cos_width, sin_width = dft_pair(width)
    cos_seq, sin_seq = dft_pair(seq_len)
    width_table = jnp.concatenate([cos_width, sin_width], axis=1).astype(jnp.bfloat16)
    seq_table = jnp.concatenate([cos_seq, -sin_seq], axis=1).astype(jnp.bfloat16)
    positions = jnp.arange(seq_len, dtype=jnp.int32)

    def spectrum(rows):
        spectral = jnp.dot(rows, width_table, preferred_element_type=jnp.float32).astype(
            jnp.bfloat16
        )
        stacked = jnp.concatenate([spectral[:, :width], spectral[:, width:]], axis=0)
        return rows.astype(jnp.float32) + jnp.dot(
            seq_table, stacked, preferred_element_type=jnp.float32
        )

    def ff_inner(rows):
        pre = jnp.dot(rows, w_first, preferred_element_type=jnp.float32) + bias_first
        active = exact_gelu(pre).astype(jnp.bfloat16)
        summed = (
            rows.astype(jnp.float32)
            + jnp.dot(active, w_second, preferred_element_type=jnp.float32)
            + bias_second
        )
        return (pre, active, summed)

    def finish(summed, mask_col):
        normed, inverse = normalize(summed)
        return ((normed * norm_gain + norm_bias) * mask_col).astype(jnp.bfloat16)

    def spare_forward(rows, mask_col):
        return jnp.zeros_like(rows)

    def mixing_forward(rows, mask_col):
        return finish(spectrum(rows), mask_col)

    def ff_forward(rows, mask_col):
        return finish(ff_inner(rows)[2], mask_col)

    def spare_backward(rows, upstream, mask_col, totals):
        return (jnp.zeros(rows.shape, jnp.float32), totals)

    def mixing_backward(rows, upstream, mask_col, totals):
        normed, inverse = normalize(spectrum(rows))
        dsum, gain_term, bias_term = norm_backward(
            upstream.astype(jnp.float32), mask_col, normed, inverse, norm_gain
        )
        dmixed = dsum.astype(jnp.bfloat16)
        dstacked = contract_rows(seq_table, dmixed).astype(jnp.bfloat16)
        dspectral = jnp.concatenate([dstacked[:seq_len], dstacked[seq_len:]], axis=1)
        grad_rows = dsum + contract_cols(dspectral, width_table)
        totals = (
            totals[0],
            totals[1],
            totals[2],
            totals[3],
            totals[4] + gain_term,
            totals[5] + bias_term,
        )
        return (grad_rows, totals)

    def ff_backward(rows, upstream, mask_col, totals):
        pre, active, summed = ff_inner(rows)
        normed, inverse = normalize(summed)
        dsum, gain_term, bias_term = norm_backward(
            upstream.astype(jnp.float32), mask_col, normed, inverse, norm_gain
        )
        dbranch = dsum.astype(jnp.bfloat16)
        grad_second = contract_rows(active, dbranch)
        dactive = contract_cols(dbranch, w_second).astype(jnp.bfloat16)
        _, gelu_back = jax.vjp(exact_gelu, pre)
        dpre = gelu_back(dactive.astype(jnp.float32))[0].astype(jnp.bfloat16)
        grad_first = contract_rows(rows, dpre)
        grad_rows = dsum + contract_cols(dpre, w_first)
        totals = (
            totals[0] + grad_first,
            totals[1] + jnp.sum(dpre.astype(jnp.float32), axis=0),
            totals[2] + grad_second,
            totals[3] + jnp.sum(dbranch.astype(jnp.float32), axis=0),
            totals[4] + gain_term,
            totals[5] + bias_term,
        )
        return (grad_rows, totals)

    def mask_for(picked):
        return (positions < lengths[picked]).astype(jnp.float32)[:, None]

    def forward_tick(tick, carry):
        incoming, kept_inputs, produced = carry
        micro = tick - section_index
        valid = (micro >= 0) & (micro < micro_count)
        picked = jnp.clip(micro, 0, micro_count - 1)
        mask_col = mask_for(picked)
        first_rows = lax.dynamic_index_in_dim(block_input, picked, 0, keepdims=False)
        first_rows = (first_rows.astype(jnp.float32) * mask_col).astype(jnp.bfloat16)
        rows = jnp.where(section_index == 0, first_rows, incoming)
        branch_index = jnp.where(valid, 1 + parity, 0)
        result = lax.switch(
            branch_index, [spare_forward, mixing_forward, ff_forward], rows, mask_col
        )
        old_input = lax.dynamic_index_in_dim(kept_inputs, picked, 0, keepdims=False)
        kept_inputs = lax.dynamic_update_index_in_dim(
            kept_inputs, jnp.where(valid, rows, old_input), picked, 0
        )
        old_output = lax.dynamic_index_in_dim(produced, picked, 0, keepdims=False)
        produced = lax.dynamic_update_index_in_dim(
            produced, jnp.where(valid, result, old_output), picked, 0
        )
        incoming = jax.tree.map(
            lambda part, own: part.astype(own.dtype),
            passed_along(as_sent(result), "section", 1),
            result,
        )
        return (incoming, kept_inputs, produced)

    blank = jnp.zeros((seq_len, width), jnp.bfloat16)
    stacked_blank = jnp.zeros(block_input.shape, jnp.bfloat16)
    _, kept_inputs, produced = lax.fori_loop(
        0, tick_count, forward_tick, (blank, stacked_blank, stacked_blank)
    )

    def backward_tick(tick, carry):
        incoming, input_grads, totals = carry
        micro = tick - (last_section - section_index)
        valid = (micro >= 0) & (micro < micro_count)
        picked = jnp.clip(micro, 0, micro_count - 1)
        mask_col = mask_for(picked)
        start_rows = lax.dynamic_index_in_dim(out_cotangent, picked, 0, keepdims=False)
        upstream = jnp.where(section_index == last_section, start_rows, incoming)
        rows = lax.dynamic_index_in_dim(kept_inputs, picked, 0, keepdims=False)
        branch_index = jnp.where(valid, 1 + parity, 0)
        grad_rows, totals = lax.switch(
            branch_index,
            [spare_backward, mixing_backward, ff_backward],
            rows,
            upstream,
            mask_col,
            totals,
        )
        old_grad = lax.dynamic_index_in_dim(input_grads, picked, 0, keepdims=False)
        input_grads = lax.dynamic_update_index_in_dim(
            input_grads, jnp.where(valid, grad_rows, old_grad), picked, 0
        )
        incoming = passed_along(grad_rows.astype(jnp.bfloat16), "section", -1)
        return (incoming, input_grads, totals)

    totals_init = (
        jnp.zeros((width, 2 * half_hidden), jnp.float32),
        jnp.zeros((2 * half_hidden,), jnp.float32),
        jnp.zeros((2 * half_hidden, width), jnp.float32),
        jnp.zeros((width,), jnp.float32),
        jnp.zeros((width,), jnp.float32),
        jnp.zeros((width,), jnp.float32),
    )
    grads_blank = jnp.zeros(block_input.shape, jnp.float32)
    _, input_grads, totals = lax.fori_loop(
        0, tick_count, backward_tick, (blank, grads_blank, totals_init)
    )
    summed = lax.psum((totals[0], totals[1], totals[2], totals[3], totals[4], totals[5]), "dp")
    lower = (
        summed[0][:, :half_hidden],
        summed[1][:half_hidden],
        summed[2][:half_hidden],
        summed[3][:half_width],
    )
    upper = (
        summed[0][:, half_hidden:],
        summed[1][half_hidden:],
        summed[2][half_hidden:],
        summed[3][half_width:],
    )
    moved = (
        passed_along(lower[0].astype(jnp.bfloat16), "section", -1).astype(jnp.float32),
        passed_along(lower[1].astype(jnp.bfloat16), "section", -1).astype(jnp.float32),
        passed_along(lower[2].astype(jnp.bfloat16), "section", -1).astype(jnp.float32),
        passed_along(lower[3].astype(jnp.bfloat16), "section", -1).astype(jnp.float32),
    )
    mine = tuple((jnp.where(parity == 1, kept, came) for kept, came in zip(upper, moved)))
    gain_grad = summed[4]
    bias_grad = summed[5]
    return (
        produced[None],
        input_grads[None],
        gain_grad[None],
        bias_grad[None],
        mine[0][None],
        mine[1][None],
        mine[2][None],
        mine[3][None],
    )


def solution(mesh):
    in_specs = (
        P("dp", None, None),
        P("dp", None, None),
        P("dp"),
        P("section", None),
        P("section", None),
        P("section", None, None),
        P("section", None),
        P("section", None, None),
        P("section", None),
    )
    out_specs = (
        P("section", "dp", None, None),
        P("section", "dp", None, None),
        P("section", None),
        P("section", None),
        P("section", None, None),
        P("section", None),
        P("section", None, None),
        P("section", None),
    )
    return jax.shard_map(
        per_device, mesh=mesh, in_specs=in_specs, out_specs=out_specs, check_vma=False
    )
```

profile of v0, /device:TPU:0, one launch (start us, length us, event | category | flops | bytes accessed | tf_op | source)
XLA Modules:
  0.0 1010.6 jit_solution(1926337576113261956)
XLA Ops:
  7.2 6.4 collective-permute-start.2
  13.6 3.5 collective-permute-start.4
  17.0 2.1 collective-permute-start.3
  19.1 1.9 collective-permute-start.5
  21.1 4.4 negate_convert_fusion
  26.6 10.0 multiply_convert_fusion.3
  36.6 1.6 pad_maximum_fusion.2
  38.3 75.3 %collective-permute-done.5 = bf16[1,384]{1,0:T(2,128)(2,1)S(1)} collective-permute-done((bf16[1,384]{1,0:T(2,128)(2,1)}, bf16[1,384]{1,0:T(2,128)(2,1)S(1)}, u32[]{:S(2)}, u32[]{:S(2)}) %collective-permute-start.5) | collective-permute-done | bytes 800 | tf_op jit(solution)/shard_map/ppermute | solution.py:14
  113.7 4.7 pad_maximum_fusion
  118.4 4.2 pad_maximum_fusion.1
  125.2 173.3 %while.50 = (s32[]{:T(128)}, bf16[512,768]{1,0:T(8,128)(2,1)S(1)}, bf16[2,512,768]{2,1,0:T(8,128)(2,1)}, bf16[2,512,768]{2,1,0:T(8,128)(2,1)}, s32[]{:T(128)}, /...) while((s32[]{:T(128)}, bf16[512,768]{1,0:T(8,128)(2,1)S(1)}, ...), condition=%wide.region_8.9_spmd.clone, body=%wide.region_0.8_spmd.clone.sunk | while | flops 4943119872 | bytes 32549844 | solution.py:198
  127.9 2.5 bitcast_dynamic-update-slice_fusion.6
  130.4 8.2 conditional.6
  130.4 3.0 convolution_convert_fusion
  134.9 2.7 fusion.110
  142.2 13.9 %collective-permute-done = bf16[512,768]{1,0:T(8,128)(2,1)S(1)} collective-permute-done((bf16[512,768]{1,0:T(8,128)(2,1)S(1)}, bf16[512,768]{1,0:T(8,128)(2,1)S(1)}, u32[]{:S(2)}, u32[]{:S(2)}) %collective-permute-start) | collective-permute-done | bytes 786464 | tf_op jit(solution)/shard_map/while/body/eval_jaxpr/ppermute | solution.py:14
  158.5 2.5 bitcast_dynamic-update-slice_fusion.6
  161.0 8.2 conditional.6
  161.0 3.0 convolution_convert_fusion
  165.6 2.7 fusion.110
  169.2 17.7 %collective-permute-start = (bf16[512,768]{1,0:T(8,128)(2,1)S(1)}, bf16[512,768]{1,0:T(8,128)(2,1)S(1)}, u32[]{:S(2)}, u32[]{:S(2)}) collective-permute-start(bf16[512,768]{1,0:T(8,128)(2,1)S(1)} %get-tuple-element.1730), channel_id=1, source_target_pairs={{0,8},{8,16},{16,24},{1,9},{9,17},{17,25},{2,10},{10,18},{18,26},{... | collective-permute-start | bytes 2359304 | tf_op jit(solution)/shard_map/while/body/eval_jaxpr/ppermute | solution.py:14
  189.2 12.9 %collective-permute-done = bf16[512,768]{1,0:T(8,128)(2,1)S(1)} collective-permute-done((bf16[512,768]{1,0:T(8,128)(2,1)S(1)}, bf16[512,768]{1,0:T(8,128)(2,1)S(1)}, u32[]{:S(2)}, u32[]{:S(2)}) %collective-permute-start) | collective-permute-done | bytes 786464 | tf_op jit(solution)/shard_map/while/body/eval_jaxpr/ppermute | solution.py:14
  204.6 2.5 bitcast_dynamic-update-slice_fusion.6
  207.1 25.9 %collective-permute-start = (bf16[512,768]{1,0:T(8,128)(2,1)S(1)}, bf16[512,768]{1,0:T(8,128)(2,1)S(1)}, u32[]{:S(2)}, u32[]{:S(2)}) collective-permute-start(bf16[512,768]{1,0:T(8,128)(2,1)S(1)} %get-tuple-element.1730), channel_id=1, source_target_pairs={{0,8},{8,16},{16,24},{1,9},{9,17},{17,25},{2,10},{10,18},{18,26},{... | collective-permute-start | bytes 2359304 | tf_op jit(solution)/shard_map/while/body/eval_jaxpr/ppermute | solution.py:14
  235.3 12.0 %collective-permute-done = bf16[512,768]{1,0:T(8,128)(2,1)S(1)} collective-permute-done((bf16[512,768]{1,0:T(8,128)(2,1)S(1)}, bf16[512,768]{1,0:T(8,128)(2,1)S(1)}, u32[]{:S(2)}, u32[]{:S(2)}) %collective-permute-start) | collective-permute-done | bytes 786464 | tf_op jit(solution)/shard_map/while/body/eval_jaxpr/ppermute | solution.py:14
  249.7 2.5 bitcast_dynamic-update-slice_fusion.6
  252.3 4.4 collective-permute-start
  259.0 11.1 %collective-permute-done = bf16[512,768]{1,0:T(8,128)(2,1)S(1)} collective-permute-done((bf16[512,768]{1,0:T(8,128)(2,1)S(1)}, bf16[512,768]{1,0:T(8,128)(2,1)S(1)}, u32[]{:S(2)}, u32[]{:S(2)}) %collective-permute-start) | collective-permute-done | bytes 786464 | tf_op jit(solution)/shard_map/while/body/eval_jaxpr/ppermute | solution.py:14
  272.5 2.5 bitcast_dynamic-update-slice_fusion.6
  275.0 10.7 %collective-permute-start = (bf16[512,768]{1,0:T(8,128)(2,1)S(1)}, bf16[512,768]{1,0:T(8,128)(2,1)S(1)}, u32[]{:S(2)}, u32[]{:S(2)}) collective-permute-start(bf16[512,768]{1,0:T(8,128)(2,1)S(1)} %get-tuple-element.1730), channel_id=1, source_target_pairs={{0,8},{8,16},{16,24},{1,9},{9,17},{17,25},{2,10},{10,18},{18,26},{... | collective-permute-start | bytes 2359304 | tf_op jit(solution)/shard_map/while/body/eval_jaxpr/ppermute | solution.py:14
  288.0 10.5 %collective-permute-done = bf16[512,768]{1,0:T(8,128)(2,1)S(1)} collective-permute-done((bf16[512,768]{1,0:T(8,128)(2,1)S(1)}, bf16[512,768]{1,0:T(8,128)(2,1)S(1)}, u32[]{:S(2)}, u32[]{:S(2)}) %collective-permute-start) | collective-permute-done | bytes 786464 | tf_op jit(solution)/shard_map/while/body/eval_jaxpr/ppermute | solution.py:14
  299.4 1.9 broadcast_in_dim.96
  301.3 4.2 broadcast_in_dim.97
  305.5 4.3 broadcast_in_dim.99
  309.8 322.8 %while.51 = (s32[]{:T(128)}, bf16[512,768]{1,0:T(8,128)(2,1)}, f32[2,512,768]{2,1,0:T(8,128)}, f32[768,3072]{0,1:T(8,128)}, f32[3072]{0:T(1024)S(1)}, /*index=5*...) while((s32[]{:T(128)}, bf16[512,768]{1,0:T(8,128)(2,1)}, ...), condition=%wide.region_27.28_spmd.clone, body=%wide.region_9.27_spmd.clone.sunk | while | flops 14648084480 | bytes 312422464 | solution.py:236
  332.0 1.5 constant_dynamic-slice_fusion.8
  334.9 12.9 %collective-permute-done.1 = bf16[512,768]{1,0:T(8,128)(2,1)} collective-permute-done((bf16[512,768]{1,0:T(8,128)(2,1)S(1)}, bf16[512,768]{1,0:T(8,128)(2,1)}, u32[]{:S(2)}, u32[]{:S(2)}) %collective-permute-start.1) | collective-permute-done | bytes 786464 | tf_op jit(solution)/shard_map/while/body/eval_jaxpr/ppermute | solution.py:14
  353.3 1.5 constant_dynamic-slice_fusion.8
  356.2 32.9 %collective-permute-done.1 = bf16[512,768]{1,0:T(8,128)(2,1)} collective-permute-done((bf16[512,768]{1,0:T(8,128)(2,1)S(1)}, bf16[512,768]{1,0:T(8,128)(2,1)}, u32[]{:S(2)}, u32[]{:S(2)}) %collective-permute-start.1) | collective-permute-done | bytes 786464 | tf_op jit(solution)/shard_map/while/body/eval_jaxpr/ppermute | solution.py:14
  397.4 129.3 %collective-permute-done.1 = bf16[512,768]{1,0:T(8,128)(2,1)} collective-permute-done((bf16[512,768]{1,0:T(8,128)(2,1)S(1)}, bf16[512,768]{1,0:T(8,128)(2,1)}, u32[]{:S(2)}, u32[]{:S(2)}) %collective-permute-start.1) | collective-permute-done | bytes 786464 | tf_op jit(solution)/shard_map/while/body/eval_jaxpr/ppermute | solution.py:14
  530.7 19.6 %conditional.7 = (f32[512,768]{1,0:T(8,128)S(1)}, f32[768,3072]{0,1:T(8,128)}, f32[3072]{0:T(1024)S(1)}, f32[3072,768]{1,0:T(8,128)}, f32[768]{0:T(1024)S(1)}, /*index=5*/f32[768]{0:T(1024)S(1)}, f32[768]{0:T(1024)S(1)}) conditional(s32[]{:T(128)} %clamp.23, (f32[768,3072]{0,1:T(8,128)}, f32[3072]{0:T(1024)S(1)}, ...), branch_computations={%region_10.10_spmd, %region_11.17_spmd, %region_18.26_spmd} | conditional | flops 14646903808 | bytes 295093664 | solution.py:212
  531.9 3.0 convolution_convert_fusion.1
  537.4 3.0 fusion.114
  541.5 2.4 fusion.68
  544.1 1.5 copy-done.7
  545.6 2.8 fusion.69
  548.4 1.9 copy.19
  554.6 40.1 %collective-permute-done.1 = bf16[512,768]{1,0:T(8,128)(2,1)} collective-permute-done((bf16[512,768]{1,0:T(8,128)(2,1)S(1)}, bf16[512,768]{1,0:T(8,128)(2,1)}, u32[]{:S(2)}, u32[]{:S(2)}) %collective-permute-start.1) | collective-permute-done | bytes 786464 | tf_op jit(solution)/shard_map/while/body/eval_jaxpr/ppermute | solution.py:14
  598.6 19.6 %conditional.7 = (f32[512,768]{1,0:T(8,128)S(1)}, f32[768,3072]{0,1:T(8,128)}, f32[3072]{0:T(1024)S(1)}, f32[3072,768]{1,0:T(8,128)}, f32[768]{0:T(1024)S(1)}, /*index=5*/f32[768]{0:T(1024)S(1)}, f32[768]{0:T(1024)S(1)}) conditional(s32[]{:T(128)} %clamp.23, (f32[768,3072]{0,1:T(8,128)}, f32[3072]{0:T(1024)S(1)}, ...), branch_computations={%region_10.10_spmd, %region_11.17_spmd, %region_18.26_spmd} | conditional | flops 14646903808 | bytes 295093664 | solution.py:212
  599.9 3.0 convolution_convert_fusion.1
  605.4 3.0 fusion.114
  609.5 2.4 fusion.68
  612.0 1.5 copy-done.7
  613.6 2.8 fusion.69
  616.4 1.9 copy.19
  622.6 9.8 collective-permute-done.1
  632.6 9.7 copy.23
  642.2 238.4 %all-reduce.4.cloned.1.call-done = (f32[768,3072]{1,0:T(8,128)}, f32[3072,768]{1,0:T(8,128)}) async-done(((f32[768,3072]{1,0:T(8,128)}, f32[3072,768]{1,0:T(8,128)}), (f32[768,3072]{1,0:T(8,128)}, f32[3072,768]{1,0:T(8,128)})) %all-reduce.4.cloned.1.call-update) | async-done | bytes 18874384 | tf_op jit(solution)/shard_map/psum | solution.py:239
  880.7 4.1 slice.78
  886.1 2.6 slice.77
  890.0 23.3 %all-reduce = (f32[1,768]{1,0:T(1,128)}, f32[1,768]{1,0:T(1,128)}, f32[3072]{0:T(1024)S(1)}, f32[768]{0:T(1024)S(1)}) all-reduce(f32[1,768]{1,0:T(1,128)S(1)} %broadcast_in_dim.101, f32[1,768]{1,0:T(1,128)S(1)} %broadcast_in_dim.102, f32[3072]{0:T(1024)S(1)} %get-tuple-element.1078, ...), channel_id=1, replica_groups=mesh['section'=4,'dp'=8] {'dp'}, use_global_device_ids=true, to_apply=%region_28.29 | all-reduce | flops 5376 | bytes 43008 | tf_op jit(solution)/shard_map/psum | solution.py:239
  915.9 74.6 %collective-permute-done.9 = bf16[384]{0:T(512)(128)(2,1)S(1)} collective-permute-done((bf16[384]{0:T(512)(128)(2,1)S(1)}, bf16[384]{0:T(512)(128)(2,1)S(1)}, u32[]{:S(2)}, u32[]{:S(2)}) %collective-permute-start.9) | collective-permute-done | bytes 800 | tf_op jit(solution)/shard_map/ppermute | solution.py:14
  991.7 6.3 fusion.95
  999.1 4.4 fusion.94
  (196 shorter events, 90.3 us)
Async XLA Ops:
  7.2 873.5 %all-reduce.4.cloned.1.call-start = ((), (), s32[]{:S(2)}) async-start(), calls=%async_computation | async-start | bytes 37748736 | tf_op jit(solution)/shard_map/psum | solution.py:239
  7.2 106.5 %collective-permute-start.2 = (bf16[1,768,1536]{2,1,0:T(8,128)(2,1)}, bf16[1,768,1536]{2,1,0:T(8,128)(2,1)}, u32[]{:S(2)}, u32[]{:S(2)}) collective-permute-start(bf16[1,768,1536]{2,1,0:T(8,128)(2,1)} %param.24), channel_id=1, source_target_pairs={{0,8},{8,16},{16,24},{1,9},{9,17},{17,25},{2,10},{10,18},{18,26},{... | collective-permute-start | bytes 7077896 | tf_op jit(solution)/shard_map/ppermute | solution.py:14
  13.6 104.9 %collective-permute-start.4 = (bf16[1,1536,768]{2,1,0:T(8,128)(2,1)}, bf16[1,1536,768]{2,1,0:T(8,128)(2,1)}, u32[]{:S(2)}, u32[]{:S(2)}) collective-permute-start(bf16[1,1536,768]{2,1,0:T(8,128)(2,1)} %param.26), channel_id=1, source_target_pairs={{0,8},{8,16},{16,24},{1,9},{9,17},{17,25},{2,10},{10,18},{18,26},{... | collective-permute-start | bytes 7077896 | tf_op jit(solution)/shard_map/ppermute | solution.py:14
  17.0 96.6 %collective-permute-start.3 = (bf16[1,1536]{1,0:T(2,128)(2,1)}, bf16[1,1536]{1,0:T(2,128)(2,1)S(1)}, u32[]{:S(2)}, u32[]{:S(2)}) collective-permute-start(bf16[1,1536]{1,0:T(2,128)(2,1)} %param.25), channel_id=1, source_target_pairs={{0,8},{8,16},{16,24},{1,9},{9,17},{17,25},{2,10},{10,18},{18,26},{... | collective-permute-start | bytes 9224 | tf_op jit(solution)/shard_map/ppermute | solution.py:14
  19.1 94.5 %collective-permute-start.5 = (bf16[1,384]{1,0:T(2,128)(2,1)}, bf16[1,384]{1,0:T(2,128)(2,1)S(1)}, u32[]{:S(2)}, u32[]{:S(2)}) collective-permute-start(bf16[1,384]{1,0:T(2,128)(2,1)} %param.27), channel_id=1, source_target_pairs={{0,8},{8,16},{16,24},{1,9},{9,17},{17,25},{2,10},{10,18},{18,26},{... | collective-permute-start | bytes 2312 | tf_op jit(solution)/shard_map/ppermute | solution.py:14
  26.6 11.6 %copy-start.12 = (bf16[1,1536]{1,0:T(2,128)(2,1)S(1)}, bf16[1,1536]{1,0:T(2,128)(2,1)}, u32[]{:S(2)}) copy-start(bf16[1,1536]{1,0:T(2,128)(2,1)} %param.25) | copy-start | bytes 9220
  26.6 11.6 %copy-start.16 = (bf16[1,384]{1,0:T(2,128)(2,1)S(1)}, bf16[1,384]{1,0:T(2,128)(2,1)}, u32[]{:S(2)}) copy-start(bf16[1,384]{1,0:T(2,128)(2,1)} %param.27) | copy-start | bytes 2308
  26.6 87.1 %copy-start.8 = (bf16[1,768,1536]{2,1,0:T(8,128)(2,1)S(1)}, bf16[1,768,1536]{2,1,0:T(8,128)(2,1)}, u32[]{:S(2)}) copy-start(bf16[1,768,1536]{2,1,0:T(8,128)(2,1)} %param.24) | copy-start | bytes 7077892
  113.7 4.7 copy-start.9
  122.6 2.6 copy-start.10
  122.6 2.6 copy-start.11
  122.6 2.6 copy-start.17
  138.6 17.5 %collective-permute-start = (bf16[512,768]{1,0:T(8,128)(2,1)S(1)}, bf16[512,768]{1,0:T(8,128)(2,1)S(1)}, u32[]{:S(2)}, u32[]{:S(2)}) collective-permute-start(bf16[512,768]{1,0:T(8,128)(2,1)S(1)} %get-tuple-element.1730), channel_id=1, source_target_pairs={{0,8},{8,16},{16,24},{1,9},{9,17},{17,25},{2,10},{10,18},{18,26},{... | collective-permute-start | bytes 2359304 | tf_op jit(solution)/shard_map/while/body/eval_jaxpr/ppermute | solution.py:14
  169.2 32.9 %collective-permute-start = (bf16[512,768]{1,0:T(8,128)(2,1)S(1)}, bf16[512,768]{1,0:T(8,128)(2,1)S(1)}, u32[]{:S(2)}, u32[]{:S(2)}) collective-permute-start(bf16[512,768]{1,0:T(8,128)(2,1)S(1)} %get-tuple-element.1730), channel_id=1, source_target_pairs={{0,8},{8,16},{16,24},{1,9},{9,17},{17,25},{2,10},{10,18},{18,26},{... | collective-permute-start | bytes 2359304 | tf_op jit(solution)/shard_map/while/body/eval_jaxpr/ppermute | solution.py:14
  207.1 40.2 %collective-permute-start = (bf16[512,768]{1,0:T(8,128)(2,1)S(1)}, bf16[512,768]{1,0:T(8,128)(2,1)S(1)}, u32[]{:S(2)}, u32[]{:S(2)}) collective-permute-start(bf16[512,768]{1,0:T(8,128)(2,1)S(1)} %get-tuple-element.1730), channel_id=1, source_target_pairs={{0,8},{8,16},{16,24},{1,9},{9,17},{17,25},{2,10},{10,18},{18,26},{... | collective-permute-start | bytes 2359304 | tf_op jit(solution)/shard_map/while/body/eval_jaxpr/ppermute | solution.py:14
  252.3 17.8 %collective-permute-start = (bf16[512,768]{1,0:T(8,128)(2,1)S(1)}, bf16[512,768]{1,0:T(8,128)(2,1)S(1)}, u32[]{:S(2)}, u32[]{:S(2)}) collective-permute-start(bf16[512,768]{1,0:T(8,128)(2,1)S(1)} %get-tuple-element.1730), channel_id=1, source_target_pairs={{0,8},{8,16},{16,24},{1,9},{9,17},{17,25},{2,10},{10,18},{18,26},{... | collective-permute-start | bytes 2359304 | tf_op jit(solution)/shard_map/while/body/eval_jaxpr/ppermute | solution.py:14
  275.0 23.4 %collective-permute-start = (bf16[512,768]{1,0:T(8,128)(2,1)S(1)}, bf16[512,768]{1,0:T(8,128)(2,1)S(1)}, u32[]{:S(2)}, u32[]{:S(2)}) collective-permute-start(bf16[512,768]{1,0:T(8,128)(2,1)S(1)} %get-tuple-element.1730), channel_id=1, source_target_pairs={{0,8},{8,16},{16,24},{1,9},{9,17},{17,25},{2,10},{10,18},{18,26},{... | collective-permute-start | bytes 2359304 | tf_op jit(solution)/shard_map/while/body/eval_jaxpr/ppermute | solution.py:14
  326.6 1.8 copy-start.13
  330.7 17.1 %collective-permute-start.1 = (bf16[512,768]{1,0:T(8,128)(2,1)S(1)}, bf16[512,768]{1,0:T(8,128)(2,1)}, u32[]{:S(2)}, u32[]{:S(2)}) collective-permute-start(bf16[512,768]{1,0:T(8,128)(2,1)S(1)} %convert_element_type.300), channel_id=1, source_target_pairs={{8,0},{16,8},{24,16},{9,1},{17,9},{25,17},{10,2},{18,10},{26,18},{... | collective-permute-start | bytes 2359304 | tf_op jit(solution)/shard_map/while/body/eval_jaxpr/ppermute | solution.py:14
  333.6 14.3 %copy-start.14 = (f32[768]{0:T(1024)S(1)}, f32[768]{0:T(1024)}, u32[]{:S(2)}) copy-start(f32[768]{0:T(1024)} %copy-done.13) | copy-start | bytes 9220 | tf_op jit(solution)/shard_map/while
  347.8 1.8 copy-start.13
  352.0 37.1 %collective-permute-start.1 = (bf16[512,768]{1,0:T(8,128)(2,1)S(1)}, bf16[512,768]{1,0:T(8,128)(2,1)}, u32[]{:S(2)}, u32[]{:S(2)}) collective-permute-start(bf16[512,768]{1,0:T(8,128)(2,1)S(1)} %convert_element_type.300), channel_id=1, source_target_pairs={{8,0},{16,8},{24,16},{9,1},{17,9},{25,17},{10,2},{18,10},{26,18},{... | collective-permute-start | bytes 2359304 | tf_op jit(solution)/shard_map/while/body/eval_jaxpr/ppermute | solution.py:14
  354.8 34.3 %copy-start.14 = (f32[768]{0:T(1024)S(1)}, f32[768]{0:T(1024)}, u32[]{:S(2)}) copy-start(f32[768]{0:T(1024)} %copy-done.13) | copy-start | bytes 9220 | tf_op jit(solution)/shard_map/while
  389.1 1.8 copy-start.13
  393.2 133.5 %collective-permute-start.1 = (bf16[512,768]{1,0:T(8,128)(2,1)S(1)}, bf16[512,768]{1,0:T(8,128)(2,1)}, u32[]{:S(2)}, u32[]{:S(2)}) collective-permute-start(bf16[512,768]{1,0:T(8,128)(2,1)S(1)} %convert_element_type.300), channel_id=1, source_target_pairs={{8,0},{16,8},{24,16},{9,1},{17,9},{25,17},{10,2},{18,10},{26,18},{... | collective-permute-start | bytes 2359304 | tf_op jit(solution)/shard_map/while/body/eval_jaxpr/ppermute | solution.py:14
  396.1 130.7 %copy-start.14 = (f32[768]{0:T(1024)S(1)}, f32[768]{0:T(1024)}, u32[]{:S(2)}) copy-start(f32[768]{0:T(1024)} %copy-done.13) | copy-start | bytes 9220 | tf_op jit(solution)/shard_map/while
  526.8 1.8 copy-start.13
  537.4 3.3 copy-start.4
  543.9 1.7 copy-start.7
  550.4 44.3 %collective-permute-start.1 = (bf16[512,768]{1,0:T(8,128)(2,1)S(1)}, bf16[512,768]{1,0:T(8,128)(2,1)}, u32[]{:S(2)}, u32[]{:S(2)}) collective-permute-start(bf16[512,768]{1,0:T(8,128)(2,1)S(1)} %convert_element_type.300), channel_id=1, source_target_pairs={{8,0},{16,8},{24,16},{9,1},{17,9},{25,17},{10,2},{18,10},{26,18},{... | collective-permute-start | bytes 2359304 | tf_op jit(solution)/shard_map/while/body/eval_jaxpr/ppermute | solution.py:14
  553.2 41.5 %copy-start.14 = (f32[768]{0:T(1024)S(1)}, f32[768]{0:T(1024)}, u32[]{:S(2)}) copy-start(f32[768]{0:T(1024)} %copy-done.13) | copy-start | bytes 9220 | tf_op jit(solution)/shard_map/while
  594.7 1.8 copy-start.13
  605.4 3.3 copy-start.4
  611.9 1.7 copy-start.7
  618.4 14.0 %collective-permute-start.1 = (bf16[512,768]{1,0:T(8,128)(2,1)S(1)}, bf16[512,768]{1,0:T(8,128)(2,1)}, u32[]{:S(2)}, u32[]{:S(2)}) collective-permute-start(bf16[512,768]{1,0:T(8,128)(2,1)S(1)} %convert_element_type.300), channel_id=1, source_target_pairs={{8,0},{16,8},{24,16},{9,1},{17,9},{25,17},{10,2},{18,10},{26,18},{... | collective-permute-start | bytes 2359304 | tf_op jit(solution)/shard_map/while/body/eval_jaxpr/ppermute | solution.py:14
  621.2 11.2 %copy-start.14 = (f32[768]{0:T(1024)S(1)}, f32[768]{0:T(1024)}, u32[]{:S(2)}) copy-start(f32[768]{0:T(1024)} %copy-done.13) | copy-start | bytes 9220 | tf_op jit(solution)/shard_map/while
  884.8 106.9 %collective-permute-start.6 = (bf16[768,1536]{1,0:T(8,128)(2,1)}, bf16[768,1536]{1,0:T(8,128)(2,1)}, u32[]{:S(2)}, u32[]{:S(2)}) collective-permute-start(bf16[768,1536]{1,0:T(8,128)(2,1)} %slice.78), channel_id=1, source_target_pairs={{8,0},{16,8},{24,16},{9,1},{17,9},{25,17},{10,2},{18,10},{26,18},{... | collective-permute-start | bytes 7077896 | tf_op jit(solution)/shard_map/ppermute | solution.py:14
  888.6 109.4 %collective-permute-start.8 = (bf16[1536,768]{1,0:T(8,128)(2,1)S(1)}, bf16[1536,768]{1,0:T(8,128)(2,1)}, u32[]{:S(2)}, u32[]{:S(2)}) collective-permute-start(bf16[1536,768]{1,0:T(8,128)(2,1)S(1)} %slice.77), channel_id=1, source_target_pairs={{8,0},{16,8},{24,16},{9,1},{17,9},{25,17},{10,2},{18,10},{26,18},{... | collective-permute-start | bytes 7077896 | tf_op jit(solution)/shard_map/ppermute | solution.py:14
  913.3 77.2 %collective-permute-start.9 = (bf16[384]{0:T(512)(128)(2,1)S(1)}, bf16[384]{0:T(512)(128)(2,1)S(1)}, u32[]{:S(2)}, u32[]{:S(2)}) collective-permute-start(bf16[384]{0:T(512)(128)(2,1)S(1)} %slice.53), channel_id=1, source_target_pairs={{8,0},{16,8},{24,16},{9,1},{17,9},{25,17},{10,2},{18,10},{26,18},{... | collective-permute-start | bytes 2312 | tf_op jit(solution)/shard_map/ppermute | solution.py:14
  914.6 76.5 %collective-permute-start.7 = (bf16[1536]{0:T(1024)(128)(2,1)S(1)}, bf16[1536]{0:T(1024)(128)(2,1)S(1)}, u32[]{:S(2)}, u32[]{:S(2)}) collective-permute-start(bf16[1536]{0:T(1024)(128)(2,1)S(1)} %slice.79), channel_id=1, source_target_pairs={{8,0},{16,8},{24,16},{9,1},{17,9},{25,17},{10,2},{18,10},{26,18},{... | collective-permute-start | bytes 9224 | tf_op jit(solution)/shard_map/ppermute | solution.py:14
  991.7 7.5 copy-start.5
Sparse Core Ops, SparseCore 0:
  642.4 238.2 all-reduce.3
where the time goes:
time: 1020 us; the launch traced here: 1010 us
  waiting for transfers between devices  674 us (66%)
  starting transfers between devices  85.6 us (8%)
  local copies, waits for them, and re-layouts  82.3 us (8%)
  other arithmetic  78.9 us (8%)
  matrix products  34.1 us (3%)
  blocking collectives  23.3 us (2%)
  loops' own time  18.1 us (2%)
  between operations  14.4 us (1%)
    ppermute x18, waiting for transfers between devices, passed_along(): return lax.ppermute(block, axis, route)  435 us
    psum x1, waiting for transfers between devices, per_device(): lax.psum((totals[0], totals[1], totals[2], totals[3], totals[4], totals[5...  238 us
    ppermute x18, starting transfers between devices, passed_along(): return lax.ppermute(block, axis, route)  85.5 us
    psum x1, blocking collectives, per_device(): lax.psum((totals[0], totals[1], totals[2], totals[3], totals[4], totals[5...  23.3 us
  transfers between devices with their start and end apart: 19, of which 13 were waited for; matrix products, arithmetic and copies ran while one was open for 6% of the time, Pallas kernels for 0%

commit v1 on v0

v1 whole, which is shorter than its diff:
```python
import functools
import math

import jax
import jax.numpy as jnp
import ml_dtypes
import numpy as np
from jax import lax
from jax.experimental import pallas as pl
from jax.experimental.pallas import tpu as pltpu
from jax.sharding import PartitionSpec as P

MESH = pl.DeviceIdType.MESH
F32, BF16 = jnp.float32, jnp.bfloat16
EPS = 1e-05
CHUNK = 128
ROOT_HALF = 1.0 / math.sqrt(2.0)
PDF_SCALE = 1.0 / math.sqrt(2.0 * math.pi)


def dft_pair(length):
    positions = np.arange(length, dtype=np.int64)
    angle = (positions[:, None] * positions[None, :] % length) * (2.0 * math.pi / length)
    scale = 1.0 / math.sqrt(length)
    return np.cos(angle) * scale, np.sin(angle) * scale


def dot(a, b):
    return jnp.dot(a, b, preferred_element_type=F32)


def dot_cols(a, b):
    return lax.dot_general(a, b, (((1,), (1,)), ((), ())), preferred_element_type=F32)


def dot_rows(a, b):
    return lax.dot_general(a, b, (((0,), (0,)), ((), ())), preferred_element_type=F32)


def gelu_pair(v):
    cdf = 0.5 * (1.0 + lax.erf(v * ROOT_HALF))
    return v * cdf, cdf + v * (jnp.exp(-0.5 * v * v) * PDF_SCALE)


def normalize(z):
    centre = z - jnp.mean(z, axis=-1, keepdims=True)
    spread = jnp.mean(centre * centre, axis=-1, keepdims=True)
    inverse = lax.rsqrt(spread + EPS)
    return centre * inverse, inverse


def norm_back(dy, normed, inverse, gain):
    e = dy * gain
    return inverse * (
        e - jnp.mean(e, axis=-1, keepdims=True) - normed * jnp.mean(e * normed, axis=-1, keepdims=True)
    )


def remote(src, dst, send, recv, device):
    return pltpu.make_async_remote_copy(
        src_ref=src, dst_ref=dst, send_sem=send, recv_sem=recv, device_id=device, device_id_type=MESH
    )


def relay(
    dp_count,
    lengths, x_hbm, cot_hbm, gain_ref, bias_ref, b_in_ref, b_out_ref, w1_hbm, w2_hbm, wt_hbm, st_hbm,
    so_hbm, ig_hbm, gw_hbm, small_ref,
    w1, w2, w1x, w2x, wt, st, hin, gin, rxa, rxb, h1, hout, dzb, gout, gmix, act, gp, actx, gpx, sp, dm,
    zacc, nrm, inv, msk, par, G, RC, R1, R2, sms, smr, smv,
    s_load, s_out, par_s, par_r, h_s, h_r, g_s, g_r, pa_s, pa_r, pb_s, pb_r,
    wz_s, wz_r, wf_s, wf_r, wc_s, wc_r, rc_s, rc_r, r1_s, r1_r, r2_s, r2_r, ag_s, ag_r, oc_s, oc_r, sm_s, sm_r,
):
    section = lax.axis_index("section")
    d = lax.axis_index("dp")
    core = lax.rem(d, 2)
    parity = lax.rem(section, 2)
    n_rows, seq, width = hin.shape
    half = w1.shape[1]
    chunks = seq // CHUNK
    tiles = half // 512
    levels = int(math.log2(dp_count)) - 1
    bits = [2 << k for k in range(levels)]

    def flipped(bit):
        return d + bit - 2 * bit * lax.rem(d // bit, 2)

    def by_core(first, second):
        return first + core * (second - first)

    bit_value = [lax.rem(d // b, 2) for b in bits]
    value = [by_core(bit_value[k], bit_value[levels - 1 - k]) for k in range(levels)]
    peer = [(section, by_core(flipped(bits[k]), flipped(bits[levels - 1 - k]))) for k in range(levels)]
    twin = (section, d + 1 - 2 * core)
    pair = (section + 1 - 2 * parity, d)
    up = (section + 1, d)
    down = (section - 1, d)

    def rows_of(t):
        return pl.ds(t * CHUNK, CHUNK)

    load_x = pltpu.make_async_copy(x_hbm, hin, s_load.at[0])
    load_cot = pltpu.make_async_copy(cot_hbm, gin, s_load.at[1])
    load_wt = pltpu.make_async_copy(wt_hbm, wt, s_load.at[2])
    load_st = pltpu.make_async_copy(st_hbm, st, s_load.at[3])
    load_w1 = pltpu.make_async_copy(w1_hbm, w1, s_load.at[4])
    load_w2 = pltpu.make_async_copy(w2_hbm, w2, s_load.at[5])

    @pl.when(section < 2)
    def _():
        load_x.start()
        load_wt.start()
        load_st.start()
        load_w1.start()
        load_w2.start()

    @pl.when(section >= 2)
    def _():
        load_w1.start()
        load_w2.start()
        load_wt.start()
        load_st.start()
        load_cot.start()

    par[parity] = jnp.zeros(par.shape[1:], F32)
    par[parity, 0:1, 0:width] = gain_ref[...]
    par[parity, 1:2, 0:width] = bias_ref[...]
    par[parity, 2:3, :] = b_in_ref[...].astype(F32)
    par[parity, 3:4, pl.ds(pl.multiple_of(parity * (width // 2), 128), width // 2)] = b_out_ref[...].astype(F32)
    smv[...] = jnp.zeros(smv.shape, F32)
    for r in range(n_rows):
        position = lax.broadcasted_iota(jnp.int32, (seq, 1), 0)
        msk[r] = jnp.where(position < lengths[r], 1.0, 0.0).astype(F32)

    barrier = pltpu.get_barrier_semaphore()

    def greet(device):
        pl.semaphore_signal(barrier, inc=1, device_id=device, device_id_type=MESH)

    greet(twin)
    for k in range(levels):
        greet(peer[k])
    pl.when(section > 0)(lambda: greet(down))
    pl.when(section < 3)(lambda: greet(up))
    pl.semaphore_wait(barrier, 1 + levels + jnp.where((section == 0) | (section == 3), 1, 2))

    swap_par = remote(par.at[parity], par.at[parity], par_s, par_r, pair)
    swap_par.start()

    quarter = half // 4
    chip = lax.rem(d // 2, 4)
    chip_far = 3 - chip
    chip_a = chip + 1 - 2 * lax.rem(chip, 2)
    chip_b = 3 - chip_a

    def part1(q):
        return pl.ds(pl.multiple_of(q * quarter, 128), quarter)

    def swap(which, q, src, send, recv, device):
        if which == 0:
            ref, to = (w1 if src == "own" else w1x), w1x
            return remote(ref.at[:, part1(q)], to.at[:, part1(q)], send, recv, device)
        ref, to = (w2 if src == "own" else w2x), w2x
        return remote(ref.at[part1(q)], to.at[part1(q)], send, recv, device)

    near_a = (section, flipped(2))
    near_b = (section, flipped(4))

    def each_core(fn):
        for which in range(2):
            pl.when(core == which)(functools.partial(fn, which))

    def weights_begin():
        load_w1.wait()
        load_w2.wait()

        def go(which):
            swap(which, chip, "own", wz_s.at[0], wz_r.at[0], pair).start()
            swap(which, chip_far, "own", wz_s.at[1], wz_r.at[1], pair).start()

        each_core(go)

    def weights_spread():
        def go(which):
            swap(which, chip, "own", wz_s.at[0], wz_r.at[0], pair).wait_recv()
            swap(which, chip, "got", wf_s.at[0], wf_r.at[0], near_a).start()
            swap(which, chip, "got", wf_s.at[1], wf_r.at[1], near_b).start()
            swap(which, chip, "got", wc_s.at[0], wc_r.at[0], twin).start()

        each_core(go)

    def weights_end():
        def go(which):
            swap(which, chip_a, "got", wf_s.at[0], wf_r.at[0], near_a).wait_recv()
            swap(which, chip_a, "got", wc_s.at[1], wc_r.at[1], twin).start()
            swap(which, chip_b, "got", wf_s.at[1], wf_r.at[1], near_b).wait_recv()
            swap(which, chip_b, "got", wc_s.at[2], wc_r.at[2], twin).start()
            swap(which, chip_far, "own", wz_s.at[1], wz_r.at[1], pair).wait_recv()
            swap(which, chip_far, "got", wc_s.at[3], wc_r.at[3], twin).start()
            other = 1 - which
            for i, q in enumerate((chip, chip_a, chip_b, chip_far)):
                swap(other, q, "got", wc_s.at[i], wc_r.at[i], twin).wait_recv()

        each_core(go)

    def weights_sent():
        def go(which):
            swap(which, chip, "own", wz_s.at[0], wz_r.at[0], pair).wait_send()
            swap(which, chip_far, "own", wz_s.at[1], wz_r.at[1], pair).wait_send()
            swap(which, chip, "got", wf_s.at[0], wf_r.at[0], near_a).wait_send()
            swap(which, chip, "got", wf_s.at[1], wf_r.at[1], near_b).wait_send()
            for i, q in enumerate((chip, chip_a, chip_b, chip_far)):
                swap(which, q, "got", wc_s.at[i], wc_r.at[i], twin).wait_send()

        each_core(go)

    def gain_of(sub):
        return par[sub, 0:1, 0:width]

    def bias_of(sub):
        return par[sub, 1:2, 0:width]

    def mix_forward(r):
        for j in range(2 * width // 512):
            cols = pl.ds(j * 512, 512)
            sp[:, cols] = dot(hin[r], wt[:, cols]).astype(BF16)
        for t in range(chunks):
            rows = rows_of(t)
            z = (
                hin[r, rows].astype(F32)
                + dot(st[rows, 0:seq], sp[:, 0:width])
                + dot(st[rows, seq : 2 * seq], sp[:, width : 2 * width])
            )
            normed, inverse = normalize(z)
            nrm[r, rows] = normed
            inv[r, rows] = inverse
            h1[r, rows] = ((normed * gain_of(0) + bias_of(0)) * msk[r, rows]).astype(BF16)

    def inner(r, w_ref, b_row, act_ref, gp_ref, at):
        for j in range(tiles):
            cols = pl.ds(j * 512, 512)
            pre = dot(h1[r], w_ref[:, cols]) + b_row(cols)
            active, slope = gelu_pair(pre)
            act_ref[at, :, cols] = active.astype(BF16)
            gp_ref[at, :, cols] = slope.astype(BF16)

    def b_own(cols):
        return par[parity, 2:3, cols]

    def b_other(cols):
        return par[1 - parity, 2:3, cols]

    def outer_bias():
        return par[0, 3:4, 0:width] + par[1, 3:4, 0:width]

    def inner_back(r, w_ref, gp_ref, at, own):
        for j in range(tiles):
            cols = pl.ds(j * 512, 512)
            dactive = dot_cols(dzb[r], w_ref[cols, :]).astype(BF16).astype(F32)
            dpre = (dactive * gp_ref[at, :, cols].astype(F32)).astype(BF16)
            gp_ref[at, :, cols] = dpre
            if own:
                smv[2:3, cols] += jnp.sum(dpre.astype(F32), axis=0, keepdims=True)

    def ff_norm_back(r, rows, upstream, normed, inverse):
        dy = upstream.astype(F32) * msk[r, rows]
        smv[4:5, 0:width] += jnp.sum(dy * normed, axis=0, keepdims=True)
        smv[5:6, 0:width] += jnp.sum(dy, axis=0, keepdims=True)
        dz = norm_back(dy, normed, inverse, gain_of(1))
        zacc[r, rows] = dz
        rounded = dz.astype(BF16)
        dzb[r, rows] = rounded
        smv[3:4, 0:width] += jnp.sum(rounded.astype(F32), axis=0, keepdims=True)

    def mix_backward(r, upstream_ref, send):
        for t in range(chunks):
            rows = rows_of(t)
            normed = nrm[r, rows]
            dy = upstream_ref[r, rows].astype(F32) * msk[r, rows]
            smv[0:1, 0:width] += jnp.sum(dy * normed, axis=0, keepdims=True)
            smv[1:2, 0:width] += jnp.sum(dy, axis=0, keepdims=True)
            dz = norm_back(dy, normed, inv[r, rows], gain_of(0))
            zacc[r, rows] = dz
            dm[rows] = dz.astype(BF16)
        for j in range(2):
            part = dot(st[:, j * seq : (j + 1) * seq], dm[...])
            sp[:, j * width : (j + 1) * width] = part.astype(BF16)
        for t in range(chunks):
            rows = rows_of(t)
            grad = (
                zacc[r, rows]
                + dot(sp[rows, 0:width], wt[:, 0:width])
                + dot(sp[rows, width : 2 * width], wt[:, width : 2 * width])
            )
            gmix[r, rows] = grad.astype(BF16)
            if send is not None:
                send(r, t)

    def send_h(r, t, src, to):
        return remote(src.at[r, rows_of(t)], hin.at[r, rows_of(t)], h_s.at[r, t], h_r.at[r, t], to)

    def send_g(r, t, src, to):
        return remote(src.at[r, rows_of(t)], gin.at[r, rows_of(t)], g_s.at[r, t], g_r.at[r, t], to)

    def send_pa(r, t):
        return remote(hout.at[r, rows_of(t)], rxa.at[r, rows_of(t)], pa_s.at[r, t], pa_r.at[r, t], pair)

    def send_pb(r, t):
        return remote(gout.at[r, rows_of(t)], rxb.at[r, rows_of(t)], pb_s.at[r, t], pb_r.at[r, t], pair)

    def each_row(fn):
        def step(r, carry):
            fn(r)
            return carry

        lax.fori_loop(0, n_rows, step, 0)

    @pl.when(section < 2)
    def _():
        load_x.wait()
        load_wt.wait()
        load_st.wait()
        swap_par.wait()
        load_w1.wait()
        load_w2.wait()

        def row(r):
            hin[r] = (hin[r].astype(F32) * msk[r]).astype(BF16)
            mix_forward(r)
            inner(r, w1, b_own, act, gp, r)

            @pl.when(section == 0)
            def _():
                for t in range(chunks):
                    rows = rows_of(t)
                    hout[r, rows] = dot(act[r, rows], w2[...]).astype(BF16)
                    send_pa(r, t).start()

            @pl.when(section == 1)
            def _():
                for t in range(chunks):
                    rows = rows_of(t)
                    zacc[r, rows] = h1[r, rows].astype(F32) + dot(act[r, rows], w2[...]) + outer_bias()
                for t in range(chunks):
                    rows = rows_of(t)
                    send_pa(r, t).wait_recv()
                    normed, inverse = normalize(zacc[r, rows] + rxa[r, rows].astype(F32))
                    nrm[r, rows] = normed
                    inv[r, rows] = inverse
                    hout[r, rows] = ((normed * gain_of(1) + bias_of(1)) * msk[r, rows]).astype(BF16)
                    send_h(r, t, hout, up).start()

        each_row(row)

    @pl.when(section >= 2)
    def _():
        weights_begin()
        load_wt.wait()
        load_st.wait()
        load_cot.wait()
        swap_par.wait()
        weights_spread()

        def row(r):
            for t in range(chunks):
                send_h(r, t, hin, up).wait_recv()

                @pl.when(section == 2)
                def _():
                    send_h(r, t, hin, up).start()

            mix_forward(r)
            inner(r, w1, b_own, act, gp, r)
            pl.when(r == 0)(weights_end)
            inner(r, w1x, b_other, actx, gpx, 0)
            for t in range(chunks):
                rows = rows_of(t)
                z = (
                    h1[r, rows].astype(F32)
                    + dot(act[r, rows], w2[...])
                    + dot(actx[0, rows], w2x[...])
                    + outer_bias()
                )
                normed, inverse = normalize(z)
                hout[r, rows] = ((normed * gain_of(1) + bias_of(1)) * msk[r, rows]).astype(BF16)
                ff_norm_back(r, rows, gin[r, rows], normed, inverse)
            inner_back(r, w2, gp, r, True)
            inner_back(r, w2x, gpx, 0, False)
            for t in range(chunks):
                rows = rows_of(t)
                grad = zacc[r, rows] + dot_cols(gp[r, rows], w1[...]) + dot_cols(gpx[0, rows], w1x[...])
                gout[r, rows] = grad.astype(BF16)

            @pl.when(section == 2)
            def _():
                mix_backward(r, gout, lambda r, t: send_g(r, t, gmix, down).start())

        each_row(row)

    def take_pb(r):
        for t in range(chunks):
            rows = rows_of(t)
            send_pb(r, t).wait_recv()
            gout[r, rows] = (zacc[r, rows] + rxb[r, rows].astype(F32)).astype(BF16)
            send_pb(r, t).start()

    @pl.when(section == 1)
    def _():
        def row(r):
            pl.when(r > 0)(lambda: take_pb(r - 1))
            for t in range(chunks):
                rows = rows_of(t)
                send_g(r, t, dzb, down).wait_recv()
                ff_norm_back(r, rows, gin[r, rows], nrm[r, rows], inv[r, rows])
                send_g(r, t, dzb, down).start()
            inner_back(r, w2, gp, r, True)
            for t in range(chunks):
                rows = rows_of(t)
                zacc[r, rows] += dot_cols(gp[r, rows], w1[...])

        each_row(row)

    @pl.when(section == 0)
    def _():
        def row(r):
            for t in range(chunks):
                rows = rows_of(t)
                send_g(r, t, dzb, up).wait_recv()
                dzb[r, rows] = gin[r, rows]
                smv[3:4, 0:width] += jnp.sum(gin[r, rows].astype(F32), axis=0, keepdims=True)
            inner_back(r, w2, gp, r, True)
            for t in range(chunks):
                rows = rows_of(t)
                gout[r, rows] = dot_cols(gp[r, rows], w1[...]).astype(BF16)
                send_pb(r, t).start()

        each_row(row)

    def store_so(src):
        return pltpu.make_async_copy(src, so_hbm, s_out.at[0])

    def store_ig(src):
        return pltpu.make_async_copy(src, ig_hbm, s_out.at[1])

    pl.when(parity == 0)(lambda: store_so(h1).start())
    pl.when(parity == 1)(lambda: store_so(hout).start())
    pl.when(section == 2)(lambda: store_ig(gmix).start())
    pl.when(section == 3)(lambda: store_ig(gout).start())

    def quarters(a, b):
        return [
            ((1 - a) * 2 + (1 - b)) * quarter,
            ((1 - a) * 2 + b) * quarter,
            (a * 2 + (1 - b)) * quarter,
            (a * 2 + b) * quarter,
        ]

    offs_1 = quarters(bit_value[0], bit_value[1])
    offs_2 = quarters(bit_value[levels - 1], bit_value[levels - 2])
    offs = [by_core(a, b) for a, b in zip(offs_1, offs_2)]
    offs_x = [by_core(b, a) for a, b in zip(offs_1, offs_2)]

    def piece(offset, count):
        return pl.ds(pl.multiple_of(offset, 16), count)

    def lanes(offset):
        return pl.ds(pl.multiple_of(offset, 128), quarter)

    def to_twin(i, offset):
        return remote(G.at[1, piece(offset, quarter)], RC.at[piece(offset, quarter)], rc_s.at[i], rc_r.at[i], twin)

    def first_hop(i):
        return remote(G.at[0, piece(offs[i], quarter)], R1.at[i], r1_s.at[i], r1_r.at[i], peer[0])

    def fold_twin(i):
        to_twin(i, offs[i]).wait_recv()
        rows = piece(offs[i], quarter)
        G[0, rows] = (G[0, rows].astype(F32) + RC[rows].astype(F32)).astype(BF16)
        if i < 2:
            first_hop(i).start()

    for i in range(4):
        grad_1 = dot_rows(gp[0, :, lanes(offs_1[i])], h1[0])
        grad_2 = dot_rows(act[0, :, lanes(offs_2[i])], dzb[0])
        for r in range(1, n_rows):
            grad_1 += dot_rows(gp[r, :, lanes(offs_1[i])], h1[r])
            grad_2 += dot_rows(act[r, :, lanes(offs_2[i])], dzb[r])
        G[core, piece(offs_1[i], quarter)] = grad_1.astype(BF16)
        G[1 - core, piece(offs_2[i], quarter)] = grad_2.astype(BF16)
        to_twin(i, offs_x[i]).start()
        if i > 0:
            fold_twin(i - 1)
    fold_twin(3)

    @pl.when(section == 1)
    def _():
        take_pb(n_rows - 1)
        store_ig(gout).start()

    def fold_first(i):
        first_hop(i).wait_recv()
        rows = piece(offs[2 + i], quarter)
        G[0, rows] = (G[0, rows].astype(F32) + R1[i].astype(F32)).astype(BF16)

    def later_hop(k, src_offset, count):
        return remote(
            G.at[0, piece(src_offset, count)], R2.at[k - 1, pl.ds(0, count)], r2_s.at[k - 1], r2_r.at[k - 1], peer[k]
        )

    fold_first(0)
    later_hop(1, offs[2], quarter).start()
    fold_first(1)
    later_hop(1, offs[2], quarter).wait_recv()
    rows = piece(offs[3], quarter)
    G[0, rows] = (G[0, rows].astype(F32) + R2[0].astype(F32)).astype(BF16)
    keep = [offs[3]]
    sent_later = [later_hop(1, offs[2], quarter)]
    count = quarter
    for k in range(2, levels):
        count //= 2
        away = keep[-1] + (1 - value[k]) * count
        keep.append(keep[-1] + value[k] * count)
        hop = later_hop(k, away, count)
        hop.start()
        hop.wait_recv()
        rows = piece(keep[-1], count)
        G[0, rows] = (G[0, rows].astype(F32) + R2[k - 1, pl.ds(0, count)].astype(F32)).astype(BF16)
        sent_later.append(hop)

    def spread(src, offset, count, i, device):
        return remote(src, gw_hbm.at[core, piece(offset, count)], ag_s.at[i], ag_r.at[i], device)

    def final_at(offset, count):
        return gw_hbm.at[core, piece(offset, count)]

    own_out = pltpu.make_async_copy(G.at[0, piece(keep[-1], count)], final_at(keep[-1], count), s_out.at[2])
    own_out.start()
    spare = []
    if levels > 2:
        own_out.wait()
        for k in range(levels - 1, 1, -1):
            mine = keep[k - 1]
            copy = spread(final_at(mine, count), mine, count, 2 + k, peer[k])
            copy.start()
            copy.wait_recv()
            spare.append(copy)
            count *= 2
        source = final_at(offs[3], quarter)
    else:
        source = G.at[0, piece(offs[3], quarter)]

    def chip_copy(i, src, offset):
        return remote(src, gw_hbm.at[core, piece(offset, quarter)], oc_s.at[i], oc_r.at[i], twin)

    own_1 = spread(source, offs[3], quarter, 0, peer[1])
    own_0 = spread(source, offs[3], quarter, 1, peer[0])
    own_1.start()
    own_0.start()
    out_3 = chip_copy(3, source, offs[3])
    out_3.start()

    @pl.when(section == 0)
    def _():
        for t in range(chunks):
            send_pb(0, t).wait_recv()
        mix_backward(0, rxb, None)

    own_1.wait_recv()
    pass_0 = spread(final_at(offs[2], quarter), offs[2], quarter, 2, peer[0])
    pass_0.start()
    out_2 = chip_copy(2, final_at(offs[2], quarter), offs[2])
    out_2.start()

    @pl.when(section == 0)
    def _():
        for r in range(1, n_rows):
            for t in range(chunks):
                send_pb(r, t).wait_recv()
            mix_backward(r, rxb, None)
        store_ig(gmix).start()

    @pl.when(parity == 1)
    def _():
        smv[0:2] = smv[4:6]

    small_hops = []
    for k in range(levels + 1):
        to = twin if k == 0 else peer[k - 1]
        sms[k] = smv[...]
        hop = remote(sms.at[k], smr.at[k], sm_s.at[k], sm_r.at[k], to)
        hop.start()
        hop.wait_recv()
        smv[...] += smr[k]
        small_hops.append(hop)
    small_ref[...] = smv[...]

    own_0.wait_recv()
    out_1 = chip_copy(1, final_at(offs[1], quarter), offs[1])
    out_1.start()
    pass_0.wait_recv()
    out_0 = chip_copy(0, final_at(offs[0], quarter), offs[0])
    out_0.start()
    for copy in (out_3, out_2, out_1, out_0):
        copy.wait_recv()

    for copy in [own_1, own_0, pass_0, out_3, out_2, out_1, out_0, first_hop(0), first_hop(1)]:
        copy.wait_send()
    for copy in sent_later + small_hops + spare:
        copy.wait_send()
    for i in range(4):
        to_twin(i, offs_x[i]).wait_send()
    if levels == 2:
        own_out.wait()
    store_so(h1).wait()
    store_ig(gout).wait()

    def sent(*makers):
        for r in range(n_rows):
            for t in range(chunks):
                for make in makers:
                    make(r, t).wait_send()

    pl.when(section == 0)(lambda: sent(send_pa, send_pb))
    pl.when(section == 1)(lambda: sent(lambda r, t: send_h(r, t, hout, up), lambda r, t: send_g(r, t, dzb, down), send_pb))

    @pl.when(section == 2)
    def _():
        sent(lambda r, t: send_h(r, t, hin, up), lambda r, t: send_g(r, t, gmix, down))

    pl.when(section >= 2)(weights_sent)


def per_device(block_input, out_cotangent, lengths, ln_gain, ln_bias, w_in, b_in, w_out, b_out):
    n_rows, seq, width = block_input.shape
    half = w_in.shape[2]
    dp_count = lax.axis_size("dp")
    levels = int(math.log2(dp_count)) - 1
    chunks = seq // CHUNK
    quarter = half // 4
    cos_w, sin_w = dft_pair(width)
    cos_s, sin_s = dft_pair(seq)
    wt = jnp.asarray(np.concatenate([cos_w, sin_w], axis=1).astype(ml_dtypes.bfloat16))
    st = jnp.asarray(np.concatenate([cos_s, -sin_s], axis=1).astype(ml_dtypes.bfloat16))
    row_block = (n_rows, seq, width)
    dma = pltpu.SemaphoreType.DMA
    vmem = pl.BlockSpec(memory_space=pltpu.VMEM)
    anywhere = pl.BlockSpec(memory_space=pl.ANY)
    by_chunk = [dma((n_rows, chunks))] * 8
    scratch = [
        pltpu.VMEM((width, half), BF16),
        pltpu.VMEM((half, width), BF16),
        pltpu.VMEM((width, half), BF16),
        pltpu.VMEM((half, width), BF16),
        pltpu.VMEM((width, 2 * width), BF16),
        pltpu.VMEM((seq, 2 * seq), BF16),
        *[pltpu.VMEM(row_block, BF16) for _ in range(9)],
        pltpu.VMEM((n_rows, seq, half), BF16),
        pltpu.VMEM((n_rows, seq, half), BF16),
        pltpu.VMEM((1, seq, half), BF16),
        pltpu.VMEM((1, seq, half), BF16),
        pltpu.VMEM((seq, 2 * width), BF16),
        pltpu.VMEM((seq, width), BF16),
        pltpu.VMEM(row_block, F32),
        pltpu.VMEM(row_block, F32),
        pltpu.VMEM((n_rows, seq, 1), F32),
        pltpu.VMEM((n_rows, seq, 1), F32),
        pltpu.VMEM((2, 8, half), F32),
        pltpu.VMEM((2, half, width), BF16),
        pltpu.VMEM((half, width), BF16),
        pltpu.VMEM((2, quarter, width), BF16),
        pltpu.VMEM((levels - 1, quarter, width), BF16),
        pltpu.VMEM((levels + 1, 8, half), F32),
        pltpu.VMEM((levels + 1, 8, half), F32),
        pltpu.VMEM((8, half), F32),
        dma((6,)),
        dma((3,)),
        dma,
        dma,
        *by_chunk,
        dma((2,)),
        dma((2,)),
        dma((2,)),
        dma((2,)),
        dma((4,)),
        dma((4,)),
        dma((4,)),
        dma((4,)),
        dma((2,)),
        dma((2,)),
        dma((levels - 1,)),
        dma((levels - 1,)),
        dma((levels + 2,)),
        dma((levels + 2,)),
        dma((4,)),
        dma((4,)),
        dma((levels + 1,)),
        dma((levels + 1,)),
    ]
    section_out, input_grad, weight_grad, small = pl.pallas_call(
        functools.partial(relay, dp_count),
        out_shape=(
            jax.ShapeDtypeStruct(row_block, BF16),
            jax.ShapeDtypeStruct(row_block, BF16),
            jax.ShapeDtypeStruct((2, half, width), BF16),
            jax.ShapeDtypeStruct((8, half), F32),
        ),
        in_specs=[
            pl.BlockSpec(memory_space=pltpu.SMEM),
            anywhere,
            anywhere,
            vmem,
            vmem,
            vmem,
            vmem,
            anywhere,
            anywhere,
            anywhere,
            anywhere,
        ],
        out_specs=(anywhere, anywhere, anywhere, vmem),
        scratch_shapes=scratch,
        compiler_params=pltpu.CompilerParams(
            collective_id=0, has_side_effects=True, vmem_limit_bytes=62 * 2**20
        ),
        name="fnet_relay",
    )(lengths, block_input, out_cotangent, ln_gain, ln_bias, b_in, b_out, w_in[0], w_out[0], wt, st)
    odd = lax.axis_index("section") % 2
    b_out_grad = lax.dynamic_slice(small, (3, odd * (width // 2)), (1, width // 2))
    return (
        section_out[None],
        input_grad.astype(F32)[None],
        small[0:1, 0:width],
        small[1:2, 0:width],
        weight_grad[0].T.astype(F32)[None],
        small[2:3, :],
        weight_grad[1].astype(F32)[None],
        b_out_grad,
    )


def solution(mesh):
    in_specs = (
        P("dp", None, None),
        P("dp", None, None),
        P("dp"),
        P("section", None),
        P("section", None),
        P("section", None, None),
        P("section", None),
        P("section", None, None),
        P("section", None),
    )
    out_specs = (
        P("section", "dp", None, None),
        P("section", "dp", None, None),
        P("section", None),
        P("section", None),
        P("section", None, None),
        P("section", None),
        P("section", None, None),
        P("section", None),
    )
    return jax.shard_map(
        per_device, mesh=mesh, in_specs=in_specs, out_specs=out_specs, check_vma=False
    )
```

time: 1020 us -> 209 us (0.20)
  waiting for transfers between devices: 674 us -> 0 us
  Pallas kernels: 0 us -> 188 us
  starting transfers between devices: 85.6 us -> 0 us
  local copies, waits for them, and re-layouts: 82.3 us -> 11.5 us
  other arithmetic: 78.9 us -> 8.73 us
  matrix products: 34.1 us -> 0 us
  blocking collectives: 23.3 us -> 0 us
  loops' own time: 18.1 us -> 0 us
  between operations: 14.4 us -> 0.67 us
    ppermute x18 -> x0, waiting for transfers between devices: 435 us -> none  [passed_along(): return lax.ppermute(block, axis, route)]
    psum x1 -> x0, waiting for transfers between devices: 238 us -> none  [per_device(): lax.psum((totals[0], totals[1], totals[2], totals[3], totals[4], totals[5...]
    pallas_call x0 -> x1, Pallas kernels: none -> 188 us  [per_device(): pl.pallas_call(functools.partial(relay, dp_count), out_shape=(jax.ShapeDt...]
    ppermute x18 -> x0, starting transfers between devices: 85.5 us -> none  [passed_along(): return lax.ppermute(block, axis, route)]
    dot_general x12 -> x0, matrix products: 34.1 us -> none  [the longest x4 12.2 us: spectrum(): jnp.dot(rows, width_table, preferred_element_type=jnp.float32)]
    dynamic_update_slice x15 -> x0, other arithmetic: 24.5 us -> none  [the longest x5 12.4 us: forward_tick(): lax.dynamic_update_index_in_dim(kept_inputs, jnp.where(valid, rows, old_i...]
    dynamic_slice x25 -> x1, local copies, waits for them, and re-layouts: 25.3 us -> 1.35 us  [per_device(): lax.dynamic_slice(small, (3, odd * (width // 2)), (1, width // 2))]
    psum x1 -> x0, blocking collectives: 23.3 us -> none  [per_device(): lax.psum((totals[0], totals[1], totals[2], totals[3], totals[4], totals[5...]
  transfers between devices with their start and end apart: 19 -> 0, of which waited for: 13 -> 0; matrix products, arithmetic and copies ran while one was open for 6% -> 0% of each run, Pallas kernels for 0% -> 0%
where the time goes in v1:
time: 209 us
  Pallas kernels  188 us (90%)
  local copies, waits for them, and re-layouts  11.5 us (6%)
  other arithmetic  8.73 us (4%)
    pallas_call x1, Pallas kernels, per_device(): pl.pallas_call(functools.partial(relay, dp_count), out_shape=(jax.ShapeDt...  188 us
    unnamed x6, local copies, waits for them, and re-layouts  7.36 us
    convert_element_type x1, other arithmetic, per_device(): weight_grad[1].astype(F32)[None]  6.83 us

profile of v1, /device:TPU:0, one launch (start us, length us, event | category | flops | bytes accessed | tf_op | source)
XLA Modules:
  0.0 208.7 jit_solution(12556964150461900697)
XLA Ops:
  0.7 187.8 %fnet_relay.1 = (bf16[2,512,768]{2,1,0:T(8,128)(2,1)}, bf16[2,512,768]{2,1,0:T(8,128)(2,1)}, bf16[2,1536,768]{2,1,0:T(8,128)(2,1)}, f32[8,1536]{1,0:T(8,128)}) custom-call(s32[2]{0:T(128)} %lengths.1, bf16[2,512,768]{2,1,0:T(8,128)(2,1)} %x_hbm.1, bf16[2,512,768]{2,1,0:T(8,128)(2,1)} %cot_hbm.1, f32[1,768]{1,0:T(1,128)} %gain_ref.1, f32[1,768]{1,0:T(1,128)} %bias_ref.1, ...), custom_call_target="tpu_custom_call" | custom-call | tf_op jit(solution)/shard_map/fnet_relay/pallas_call | solution.py:699
  188.5 1.3 constant_dynamic-slice_fusion
  189.8 1.4 fusion
  191.2 1.4 slice.18
  192.6 6.8 %slice_convert_fusion = (f32[1,1536,768]{2,1,0:T(8,128)}, f32[1,768,1536]{1,2,0:T(8,128)}) fusion(bf16[2,1536,768]{2,1,0:T(8,128)(2,1)} %get-tuple-element.15), kind=kLoop, calls=%fused_computation.1 | loop fusion | flops 2359296 | bytes 14155776 | tf_op jit(solution)/shard_map/convert_element_type | solution.py:736
  199.5 0.0 copy-start.1
  199.5 6.2 %copy.19 = f32[1,768,1536]{2,1,0:T(8,128)} copy(f32[1,768,1536]{1,2,0:T(8,128)} %get-tuple-element.25) | data formatting | bytes 9437184
  205.6 0.0 copy-done.1
  205.6 0.0 copy-start
  205.6 1.9 bitcast_convert_fusion
  207.5 0.1 copy-done
  207.6 1.1 copy.21
Async XLA Ops:
  199.5 6.2 %copy-start.1 = (bf16[2,512,768]{2,1,0:T(8,128)(2,1)S(1)}, bf16[2,512,768]{2,1,0:T(8,128)(2,1)}, u32[]{:S(2)}) copy-start(bf16[2,512,768]{2,1,0:T(8,128)(2,1)} %get-tuple-element.13) | copy-start | bytes 4718596
  205.6 2.0 copy-start

commit v2 on v1

v2 whole, which is shorter than its diff:
```python
import functools
import math

import jax
import jax.numpy as jnp
import ml_dtypes
import numpy as np
from jax import lax
from jax.experimental import pallas as pl
from jax.experimental.pallas import tpu as pltpu
from jax.sharding import PartitionSpec as P

MESH = pl.DeviceIdType.MESH
F32, BF16 = jnp.float32, jnp.bfloat16
EPS = 1e-05
CHUNK = 128
WIDE = 2
ROOT_HALF = 1.0 / math.sqrt(2.0)
PDF_SCALE = 1.0 / math.sqrt(2.0 * math.pi)


def dft_pair(length):
    positions = np.arange(length, dtype=np.int64)
    angle = (positions[:, None] * positions[None, :] % length) * (2.0 * math.pi / length)
    scale = 1.0 / math.sqrt(length)
    return np.cos(angle) * scale, np.sin(angle) * scale


def dot(a, b):
    return jnp.dot(a, b, preferred_element_type=F32)


def dot_cols(a, b):
    return lax.dot_general(a, b, (((1,), (1,)), ((), ())), preferred_element_type=F32)


def dot_rows(a, b):
    return lax.dot_general(a, b, (((0,), (0,)), ((), ())), preferred_element_type=F32)


def gelu_pair(v):
    cdf = 0.5 * (1.0 + lax.erf(v * ROOT_HALF))
    return v * cdf, cdf + v * (jnp.exp(-0.5 * v * v) * PDF_SCALE)


def normalize(z):
    centre = z - jnp.mean(z, axis=-1, keepdims=True)
    spread = jnp.mean(centre * centre, axis=-1, keepdims=True)
    inverse = lax.rsqrt(spread + EPS)
    return centre * inverse, inverse


def norm_back(dy, normed, inverse, gain):
    e = dy * gain
    return inverse * (
        e - jnp.mean(e, axis=-1, keepdims=True) - normed * jnp.mean(e * normed, axis=-1, keepdims=True)
    )


def remote(src, dst, send, recv, device):
    return pltpu.make_async_remote_copy(
        src_ref=src, dst_ref=dst, send_sem=send, recv_sem=recv, device_id=device, device_id_type=MESH
    )


def relay(
    dp_count,
    lengths, x_hbm, cot_hbm, gain_ref, bias_ref, b_in_ref, b_out_ref, w1_hbm, w2_hbm, wt_hbm, st_hbm,
    so_hbm, ig_hbm, gw_hbm, small_ref,
    w1, w2, w1x, w2x, wt, st, hin, gin, rxa, rxb, h1, hout, dzb, gout, gmix, act, gp, actx, gpx, sp, dm,
    zacc, nrm, inv, msk, par, G, RC, R1, R2, sms, smr, smv,
    turn, s_load, s_out, par_s, par_r, h_s, h_r, g_s, g_r, pa_s, pa_r, pb_s, pb_r,
    wz_s, wz_r, wa_s, wa_r, wb_s, wb_r, wc_s, wc_r, rc_s, rc_r, r1_s, r1_r, r2_s, r2_r, ag_s, ag_r, oc_s, oc_r, lo_s, lo_r, sm_s, sm_r,
):
    section = lax.axis_index("section")
    d = lax.axis_index("dp")
    core = lax.rem(d, 2)
    parity = lax.rem(section, 2)
    n_rows, seq, width = hin.shape
    half = w1.shape[1]
    chunks = seq // CHUNK
    tiles = half // 512
    levels = int(math.log2(dp_count)) - 1
    bits = [2 << k for k in range(levels)]

    def flipped(bit):
        return d + bit - 2 * bit * lax.rem(d // bit, 2)

    def by_core(first, second):
        return first + core * (second - first)

    bit_value = [lax.rem(d // b, 2) for b in bits]
    value = [by_core(bit_value[k], bit_value[levels - 1 - k]) for k in range(levels)]
    peer = [(section, by_core(flipped(bits[k]), flipped(bits[levels - 1 - k]))) for k in range(levels)]
    twin = (section, d + 1 - 2 * core)
    pair = (section + 1 - 2 * parity, d)
    up = (section + 1, d)
    down = (section - 1, d)

    def rows_of(t):
        return pl.ds(t * CHUNK, CHUNK)

    wide_rows = [pl.ds(i * WIDE * CHUNK, WIDE * CHUNK) for i in range(chunks // WIDE)]

    barrier = pltpu.get_barrier_semaphore()

    def greet(device):
        pl.semaphore_signal(barrier, inc=1, device_id=device, device_id_type=MESH)

    greet(twin)
    for k in range(levels):
        greet(peer[k])
    pl.when(section > 0)(lambda: greet(down))
    pl.when(section < 3)(lambda: greet(up))

    load_x = pltpu.make_async_copy(x_hbm, hin, s_load.at[0])
    load_cot = pltpu.make_async_copy(cot_hbm, gin, s_load.at[1])
    load_wt = pltpu.make_async_copy(wt_hbm, wt, s_load.at[2])
    load_st = pltpu.make_async_copy(st_hbm, st, s_load.at[3])
    load_w1 = pltpu.make_async_copy(w1_hbm, w1, s_load.at[4])
    load_w2 = pltpu.make_async_copy(w2_hbm, w2, s_load.at[5])

    @pl.when(section < 2)
    def _():
        load_x.start()
        load_wt.start()
        load_st.start()
        load_w1.start()
        load_w2.start()

    @pl.when(section >= 2)
    def _():
        load_w1.start()
        load_w2.start()
        load_wt.start()
        load_st.start()
        load_cot.start()

    par[parity] = jnp.zeros(par.shape[1:], F32)
    par[parity, 0:1, 0:width] = gain_ref[...]
    par[parity, 1:2, 0:width] = bias_ref[...]
    par[parity, 2:3, :] = b_in_ref[...].astype(F32)
    par[parity, 3:4, pl.ds(pl.multiple_of(parity * (width // 2), 128), width // 2)] = b_out_ref[...].astype(F32)
    smv[...] = jnp.zeros(smv.shape, F32)
    for r in range(n_rows):
        position = lax.broadcasted_iota(jnp.int32, (seq, 1), 0)
        msk[r] = jnp.where(position < lengths[r], 1.0, 0.0).astype(F32)

    pl.semaphore_wait(barrier, 1 + levels + jnp.where((section == 0) | (section == 3), 1, 2))

    swap_par = remote(par.at[parity], par.at[parity], par_s, par_r, pair)
    swap_par.start()

    quarter = half // 4
    chip = lax.rem(d // 2, 4)
    chip_far = 3 - chip
    chip_a = chip + 1 - 2 * lax.rem(chip, 2)
    chip_b = 3 - chip_a
    near_a = (section, flipped(2))
    near_b = (section, flipped(4))

    def swap(which, q, i, n, own, send, recv, device):
        if which == 0:
            from_ref, to_ref = (w1_hbm if own else w1x), w1x
        else:
            from_ref, to_ref = (w2_hbm if own else w2x), w2x
        third = to_ref.shape[0] // 12
        part = pl.ds(pl.multiple_of((3 * q + i) * third, 16), n * third)
        return remote(from_ref.at[part], to_ref.at[part], send, recv, device)

    def each_core(fn):
        for which in range(2):
            pl.when(core == which)(functools.partial(fn, which))

    def z_hop(which, i):
        if i < 3:
            return swap(which, chip, i, 1, True, wz_s.at[i], wz_r.at[i], pair)
        return swap(which, chip_far, 0, 1, True, wz_s.at[3], wz_r.at[3], pair)

    def a_hop(which, i):
        if i < 3:
            return swap(which, chip, i, 1, False, wa_s.at[i], wa_r.at[i], near_a)
        return swap(which, chip_b, 1, 1, False, wa_s.at[3], wa_r.at[3], near_a)

    def b_hop(which, i):
        if i < 3:
            return swap(which, chip, i, 1, False, wb_s.at[i], wb_r.at[i], near_b)
        return swap(which, chip_a, 2, 1, False, wb_s.at[3], wb_r.at[3], near_b)

    def a_got(which, i):
        if i < 3:
            return swap(which, chip_a, i, 1, False, wa_s.at[i], wa_r.at[i], near_a)
        return swap(which, chip_far, 1, 1, False, wa_s.at[3], wa_r.at[3], near_a)

    def b_got(which, i):
        if i < 3:
            return swap(which, chip_b, i, 1, False, wb_s.at[i], wb_r.at[i], near_b)
        return swap(which, chip_far, 2, 1, False, wb_s.at[3], wb_r.at[3], near_b)

    def twin_hop(which, i):
        q = (chip, chip_a, chip_b, chip_far)[i]
        return swap(which, q, 0, 3, False, wc_s.at[i], wc_r.at[i], twin)

    def weights_begin():
        def go(which):
            for i in range(4):
                z_hop(which, i).start()

        each_core(go)

    def weights_spread():
        def go(which):
            for i in range(3):
                z_hop(which, i).wait_recv()
                a_hop(which, i).start()
                b_hop(which, i).start()
            twin_hop(which, 0).start()
            b_got(which, 0).wait_recv()
            b_got(which, 1).wait_recv()
            a_hop(which, 3).start()
            for i in range(3):
                a_got(which, i).wait_recv()
            b_hop(which, 3).start()
            twin_hop(which, 1).start()

        each_core(go)

    def weights_end():
        def go(which):
            b_got(which, 2).wait_recv()
            twin_hop(which, 2).start()
            z_hop(which, 3).wait_recv()
            a_got(which, 3).wait_recv()
            b_got(which, 3).wait_recv()
            twin_hop(which, 3).start()

        each_core(go)

    def weights_ready():
        def go(which):
            for i in range(4):
                twin_hop(1 - which, i).wait_recv()

        each_core(go)

    def weights_sent():
        def go(which):
            for i in range(4):
                pl.when(section > 0)(z_hop(which, i).wait_send)

                @pl.when(section != 1)
                def _():
                    a_hop(which, i).wait_send()
                    b_hop(which, i).wait_send()
                    twin_hop(which, i).wait_send()

        each_core(go)

    def gain_of(sub):
        return par[sub, 0:1, 0:width]

    def bias_of(sub):
        return par[sub, 1:2, 0:width]

    def mix_forward(r):
        for j in range(2 * width // 512):
            cols = pl.ds(j * 512, 512)
            sp[:, cols] = dot(hin[r], wt[:, cols]).astype(BF16)
        for t in range(chunks):
            rows = rows_of(t)
            z = (
                hin[r, rows].astype(F32)
                + dot(st[rows, 0:seq], sp[:, 0:width])
                + dot(st[rows, seq : 2 * seq], sp[:, width : 2 * width])
            )
            normed, inverse = normalize(z)
            nrm[r, rows] = normed
            inv[r, rows] = inverse
            h1[r, rows] = ((normed * gain_of(0) + bias_of(0)) * msk[r, rows]).astype(BF16)

    def inner(r, w_ref, b_row, act_ref, act_at, gp_ref):
        for j in range(tiles):
            cols = pl.ds(j * 512, 512)
            for t in range(chunks):
                rows = rows_of(t)
                pre = dot(h1[r, rows], w_ref[:, cols]) + b_row(cols)
                active, slope = gelu_pair(pre)
                act_ref[act_at, rows, cols] = active.astype(BF16)
                gp_ref[r, rows, cols] = slope.astype(BF16)

    def b_own(cols):
        return par[parity, 2:3, cols]

    def b_other(cols):
        return par[1 - parity, 2:3, cols]

    def outer_bias():
        return par[0, 3:4, 0:width] + par[1, 3:4, 0:width]

    def inner_back(r, w_ref, gp_ref, own):
        for j in range(tiles):
            cols = pl.ds(j * 512, 512)
            dactive = dot_cols(dzb[r], w_ref[cols, :]).astype(BF16).astype(F32)
            dpre = (dactive * gp_ref[r, :, cols].astype(F32)).astype(BF16)
            gp_ref[r, :, cols] = dpre
            if own:
                smv[2:3, cols] += jnp.sum(dpre.astype(F32), axis=0, keepdims=True)

    def ff_norm_back(r, rows, upstream, normed, inverse):
        dy = upstream.astype(F32) * msk[r, rows]
        smv[4:5, 0:width] += jnp.sum(dy * normed, axis=0, keepdims=True)
        smv[5:6, 0:width] += jnp.sum(dy, axis=0, keepdims=True)
        dz = norm_back(dy, normed, inverse, gain_of(1))
        zacc[r, rows] = dz
        rounded = dz.astype(BF16)
        dzb[r, rows] = rounded
        smv[3:4, 0:width] += jnp.sum(rounded.astype(F32), axis=0, keepdims=True)

    def mix_backward(r, upstream_ref):
        for t in range(chunks):
            rows = rows_of(t)
            normed = nrm[r, rows]
            dy = upstream_ref[r, rows].astype(F32) * msk[r, rows]
            smv[0:1, 0:width] += jnp.sum(dy * normed, axis=0, keepdims=True)
            smv[1:2, 0:width] += jnp.sum(dy, axis=0, keepdims=True)
            dz = norm_back(dy, normed, inv[r, rows], gain_of(0))
            zacc[r, rows] = dz
            dm[rows] = dz.astype(BF16)
        for j in range(2):
            part = dot(st[:, j * seq : (j + 1) * seq], dm[...])
            sp[:, j * width : (j + 1) * width] = part.astype(BF16)
        for t in range(chunks):
            rows = rows_of(t)
            grad = (
                zacc[r, rows]
                + dot(sp[rows, 0:width], wt[:, 0:width])
                + dot(sp[rows, width : 2 * width], wt[:, width : 2 * width])
            )
            gmix[r, rows] = grad.astype(BF16)
            pl.when(section == 2)(send_g(r, t, gmix, down).start)

    def send_h(r, t, src, to):
        return remote(src.at[r, rows_of(t)], hin.at[r, rows_of(t)], h_s.at[r, t], h_r.at[r, t], to)

    def send_g(r, t, src, to):
        return remote(src.at[r, rows_of(t)], gin.at[r, rows_of(t)], g_s.at[r, t], g_r.at[r, t], to)

    def send_pa(r, t):
        return remote(hout.at[r, rows_of(t)], rxa.at[r, rows_of(t)], pa_s.at[r, t], pa_r.at[r, t], pair)

    def send_pb(r, t, src):
        return remote(src.at[r, rows_of(t)], rxb.at[r, rows_of(t)], pb_s.at[r, t], pb_r.at[r, t], pair)

    first_layer = section < 2
    whole = section != 1

    def finish_with_pair(r):
        for t in range(chunks):
            rows = rows_of(t)
            send_pa(r, t).wait_recv()
            normed, inverse = normalize(zacc[r, rows] + rxa[r, rows].astype(F32))
            nrm[r, rows] = normed
            inv[r, rows] = inverse
            hout[r, rows] = ((normed * gain_of(1) + bias_of(1)) * msk[r, rows]).astype(BF16)
            send_h(r, t, hout, up).start()

    def row_forward(r):
        @pl.when(first_layer)
        def _():
            hin[r] = (hin[r].astype(F32) * msk[r]).astype(BF16)

        @pl.when(jnp.logical_not(first_layer))
        def _():
            for t in range(chunks):
                send_h(r, t, hin, up).wait_recv()
                pl.when(section == 2)(send_h(r, t, hin, up).start)

        mix_forward(r)
        inner(r, w1, b_own, act, r, gp)

        @pl.when(first_layer)
        def _():
            for t in range(chunks):
                rows = rows_of(t)
                part = dot(act[r, rows], w2[...])

                @pl.when(section == 0)
                def _():
                    hout[r, rows] = part.astype(BF16)
                    pl.when((core == 0) & (r == 0))(send_pa(r, t).start)

                @pl.when(section == 1)
                def _():
                    zacc[r, rows] = h1[r, rows].astype(F32) + part + outer_bias()

        pl.when(section == 1)(lambda: finish_with_pair(r))

    def send_row(r):
        for t in range(chunks):
            send_pa(r, t).start()

    def half_sent(r):
        for t in range(chunks // 2):
            send_pa(r, t).wait_send()

    def hand_over(r):
        half_sent(r)
        pl.semaphore_signal(turn, inc=1, device_id=twin, device_id_type=MESH)

    def take_turns():
        @pl.when(core == 0)
        def _():
            hand_over(0)
            for r in range(1, n_rows):
                pl.semaphore_wait(turn, 1)
                send_row(r)
                hand_over(r)

        @pl.when(core == 1)
        def _():
            for r in range(n_rows):
                pl.semaphore_wait(turn, 1)
                send_row(r)
                (hand_over if r < n_rows - 1 else half_sent)(r)

    def part_back(r):
        for i, rows in enumerate(wide_rows):
            part = dot_cols(gp[r, rows], w1[...])

            @pl.when(section == 0)
            def _():
                zacc[r, rows] = dzb[r, rows].astype(F32)
                rxa[r, rows] = part.astype(BF16)
                for t in range(i * WIDE, (i + 1) * WIDE):
                    send_pb(r, t, rxa).start()

            zacc[r, rows] += part

            @pl.when(whole)
            def _():
                gout[r, rows] = (zacc[r, rows] + dot_cols(gpx[r, rows], w1x[...])).astype(BF16)

    def row_backward(r):
        pl.when((section == 0) & (r == 0))(weights_spread)
        pl.when(((section == 0) | ((section > 1) & (core == 0))) & (r == 0))(weights_end)
        pl.when(whole & (r == 0))(weights_ready)
        pl.when(whole)(lambda: inner(r, w1x, b_other, actx, 0, gpx))

        @pl.when(section == 0)
        def _():
            for t in range(chunks):
                rows = rows_of(t)
                send_g(r, t, dzb, up).wait_recv()
                dzb[r, rows] = gin[r, rows]
                smv[3:4, 0:width] += jnp.sum(gin[r, rows].astype(F32), axis=0, keepdims=True)

        @pl.when(section == 1)
        def _():
            for t in range(chunks):
                rows = rows_of(t)
                send_g(r, t, dzb, down).wait_recv()
                ff_norm_back(r, rows, gin[r, rows], nrm[r, rows], inv[r, rows])
                send_g(r, t, dzb, down).start()

        @pl.when(jnp.logical_not(first_layer))
        def _():
            for t in range(chunks):
                rows = rows_of(t)
                z = (
                    h1[r, rows].astype(F32)
                    + dot(act[r, rows], w2[...])
                    + dot(actx[0, rows], w2x[...])
                    + outer_bias()
                )
                normed, inverse = normalize(z)
                hout[r, rows] = ((normed * gain_of(1) + bias_of(1)) * msk[r, rows]).astype(BF16)
                ff_norm_back(r, rows, gin[r, rows], normed, inverse)

        inner_back(r, w2, gp, True)

        pl.when(whole)(lambda: inner_back(r, w2x, gpx, False))

    def join_parts(r, to):
        for t in range(chunks):
            rows = rows_of(t)
            send_pb(r, t, rxa).wait_recv()
            to[r, rows] = (zacc[r, rows] + rxb[r, rows].astype(F32)).astype(BF16)

    pl.when(section > 0)(weights_begin)
    load_wt.wait()
    load_st.wait()
    load_w1.wait()
    load_w2.wait()
    swap_par.wait()

    @pl.when(first_layer)
    def _():
        load_x.wait()

    @pl.when(jnp.logical_not(first_layer))
    def _():
        load_cot.wait()
        weights_spread()
        pl.when(core == 1)(weights_end)

    def store_so(src):
        return pltpu.make_async_copy(src, so_hbm, s_out.at[0])

    def store_ig(src):
        return pltpu.make_async_copy(src, ig_hbm, s_out.at[1])

    def store_ready():
        pl.when(parity == 0)(lambda: store_so(h1).start())
        pl.when(parity == 1)(lambda: store_so(hout).start())
        pl.when(section == 2)(lambda: store_ig(gmix).start())
        pl.when(section == 3)(lambda: store_ig(gout).start())

    def place(a, b, i):
        first, second = i // 2, lax.rem(i, 2)
        return ((1 - a + first * (2 * a - 1)) * 2 + 1 - b + second * (2 * b - 1)) * quarter

    def place_1(i):
        return place(bit_value[0], bit_value[1], i)

    def place_2(i):
        return place(bit_value[levels - 1], bit_value[levels - 2], i)

    def place_own(i):
        return by_core(place_1(i), place_2(i))

    def place_twin(i):
        return by_core(place_2(i), place_1(i))

    offs = [place_own(i) for i in range(4)]

    def piece(offset, count):
        return pl.ds(pl.multiple_of(offset, 16), count)

    def lanes(offset):
        return pl.ds(pl.multiple_of(offset, 128), quarter)

    def to_twin(i, offset):
        return remote(G.at[1, piece(offset, quarter)], RC.at[piece(offset, quarter)], rc_s.at[i], rc_r.at[i], twin)

    def first_hop(i):
        return remote(G.at[0, piece(place_own(i), quarter)], R1.at[i], r1_s.at[i], r1_r.at[i], peer[0])

    def fold_twin(i):
        to_twin(i, place_own(i)).wait_recv()
        rows = piece(place_own(i), quarter)
        G[0, rows] = (G[0, rows].astype(F32) + RC[rows].astype(F32)).astype(BF16)

    def grads_quarter(i):
        at_1, at_2 = place_1(i), place_2(i)
        grad_1 = dot_rows(gp[0, :, lanes(at_1)], h1[0])
        grad_2 = dot_rows(act[0, :, lanes(at_2)], dzb[0])
        for r in range(1, n_rows):
            grad_1 += dot_rows(gp[r, :, lanes(at_1)], h1[r])
            grad_2 += dot_rows(act[r, :, lanes(at_2)], dzb[r])
        G[core, piece(at_1, quarter)] = grad_1.astype(BF16)
        G[1 - core, piece(at_2, quarter)] = grad_2.astype(BF16)
        to_twin(i, place_twin(i)).start()

    def grads():
        for i in range(4):
            pl.when(section > 0)(lambda: small_begin(i) if i <= levels else None)
            grads_quarter(i)
            if i > 0:
                fold_twin(i - 1)
            if 1 <= i < 3:
                first_hop(i - 1).start()
            pl.when(section > 0)(lambda: small_end(i) if i <= levels else None)
        fold_twin(3)

    def fold_first(i):
        first_hop(i).wait_recv()
        rows = piece(offs[2 + i], quarter)
        G[0, rows] = (G[0, rows].astype(F32) + R1[i].astype(F32)).astype(BF16)

    def later_hop(k):
        count = quarter >> (k - 1)
        return remote(
            G.at[0, piece(away[k], count)], R2.at[k - 1, pl.ds(0, count)], r2_s.at[k - 1], r2_r.at[k - 1], peer[k]
        )

    def fold_later(k):
        count = quarter >> (k - 1)
        later_hop(k).wait_recv()
        rows = piece(keep[k], count)
        G[0, rows] = (G[0, rows].astype(F32) + R2[k - 1, pl.ds(0, count)].astype(F32)).astype(BF16)

    keep, away = {1: offs[3]}, {1: offs[2]}
    for k in range(2, levels):
        count = quarter >> (k - 1)
        keep[k] = keep[k - 1] + value[k] * count
        away[k] = keep[k - 1] + (1 - value[k]) * count
    least = quarter >> (levels - 2)

    def spread(src, offset, count, i, device):
        return remote(src, gw_hbm.at[core, piece(offset, count)], ag_s.at[i], ag_r.at[i], device)

    def final_at(offset, count):
        return gw_hbm.at[core, piece(offset, count)]

    own_out = pltpu.make_async_copy(G.at[0, piece(keep[levels - 1], least)], final_at(keep[levels - 1], least), s_out.at[2])

    def wider(k):
        count = quarter >> (k - 1)
        return spread(final_at(keep[k], count), keep[k], count, 7 + k, peer[k])

    def chip_copy(i):
        src = source if i == 3 else final_at(offs[i], quarter)
        return remote(src, final_at(offs[i], quarter), oc_s.at[i], oc_r.at[i], twin)

    source = final_at(offs[3], quarter) if levels > 2 else G.at[0, piece(offs[3], quarter)]
    third = quarter // 3

    def own_to(k, i):
        src = source.at[pl.ds(i * third, third)]
        return spread(src, offs[3] + i * third, third, (1 - k) * 3 + i, peer[k])

    def pass_on(i):
        begin = offs[2] + i * third
        return spread(final_at(begin, third), begin, third, 6 + i, peer[0])

    def last_out(i):
        begin = offs[0] + i * third
        return remote(final_at(begin, third), final_at(begin, third), lo_s.at[i], lo_r.at[i], twin)

    def small_hop(k):
        return remote(sms.at[k], smr.at[k], sm_s.at[k], sm_r.at[k], twin if k == 0 else peer[k - 1])

    def small_begin(k):
        sms[k] = smv[...]
        small_hop(k).start()

    def small_end(k):
        small_hop(k).wait_recv()
        smv[...] += smr[k]

    def small_sum(begin=0):
        for k in range(begin, levels + 1):
            small_begin(k)
            small_end(k)

    def sum_first():
        def small(*calls):
            @pl.when(section == 0)
            def _():
                for call, k in calls:
                    call(k)

        small((small_begin, 0))
        fold_first(0)
        later_hop(1).start()
        small((small_end, 0))
        fold_first(1)
        small((small_begin, 1), (small_end, 1), (small_begin, 2))
        fold_later(1)
        small((small_end, 2))
        for k in range(2, levels):
            later_hop(k).start()
            fold_later(k)
        own_out.start()
        if levels > 2:
            own_out.wait()
            for k in range(levels - 1, 1, -1):
                wider(k).start()
                wider(k).wait_recv()

        pl.when(section == 0)(lambda: small_sum(3))
        pl.when(section > 0)(lambda: small_sum(4))
        for i in range(3):
            own_to(1, i).start()
            own_to(0, i).start()
        chip_copy(3).start()

    def sum_next():
        for i in range(3):
            own_to(1, i).wait_recv()
            pass_on(i).start()
        chip_copy(2).start()


    def step(i, carry):
        forward = jnp.where(first_layer, i < n_rows, lax.rem(i, 2) == 0) & (i < 2 * n_rows)
        backward = jnp.where(first_layer, i >= n_rows, lax.rem(i, 2) == 1) & (i < 2 * n_rows)
        r = jnp.where(first_layer, lax.rem(i, n_rows), lax.rem(i // 2, n_rows))
        last = i == 2 * n_rows

        pl.when(forward)(lambda: row_forward(r))
        pl.when((section == 0) & (i == n_rows - 1))(take_turns)
        pl.when(backward)(lambda: row_backward(r))

        @pl.when(last)
        def _():
            store_ready()

            @pl.when(parity == 1)
            def _():
                smv[0:2] = smv[4:6]

            grads()

        late = first_layer & last
        pl.when((backward & jnp.logical_not(first_layer & (r == n_rows - 1))) | late)(
            lambda: part_back(jnp.where(late, n_rows - 1, r))
        )

        now = jnp.where(late, n_rows - 1, r)
        in_turn = backward & jnp.logical_not(first_layer & (r == n_rows - 1))
        pl.when(((section == 2) & in_turn) | ((section == 0) & (in_turn | late)))(lambda: mix_backward(now, gout))
        return carry

    lax.fori_loop(0, 2 * n_rows + 1, step, 0)

    @pl.when(section == 0)
    def _():
        store_ig(gmix).start()

    sum_first()
    sum_next()

    @pl.when(section == 1)
    def _():
        for r in range(n_rows):
            join_parts(r, gmix)
        store_ig(gmix).start()

    small_ref[...] = smv[...]
    small_ref[3:4, 0 : width // 2] = smv[3:4, pl.ds(pl.multiple_of(parity * (width // 2), 128), width // 2)]

    for i in range(3):
        own_to(0, i).wait_recv()
    chip_copy(1).start()
    for i in range(3):
        pass_on(i).wait_recv()
        last_out(i).start()
    for i in range(1, 4):
        chip_copy(i).wait_recv()
    for i in range(3):
        last_out(i).wait_recv()

    for copy in [chip_copy(3), chip_copy(2), chip_copy(1), first_hop(0), first_hop(1)]:
        copy.wait_send()
    for k in range(1, levels):
        later_hop(k).wait_send()
        if k > 1:
            wider(k).wait_send()
    for i in range(3):
        for copy in (own_to(1, i), own_to(0, i), pass_on(i), last_out(i)):
            copy.wait_send()
    for k in range(levels + 1):
        small_hop(k).wait_send()
    for i in range(4):
        to_twin(i, place_twin(i)).wait_send()
    if levels == 2:
        own_out.wait()
    store_so(h1).wait()
    store_ig(gout).wait()

    def sent(*makers):
        for r in range(n_rows):
            for t in range(chunks):
                for make in makers:
                    make(r, t).wait_send()

    pl.when(section == 0)(lambda: sent(lambda r, t: send_pb(r, t, rxa)))

    @pl.when(section == 0)
    def _():
        for r in range(n_rows):
            for t in range(chunks // 2, chunks):
                send_pa(r, t).wait_send()

    pl.when(section == 1)(lambda: sent(lambda r, t: send_h(r, t, hout, up), lambda r, t: send_g(r, t, dzb, down)))

    @pl.when(section == 2)
    def _():
        sent(lambda r, t: send_h(r, t, hin, up), lambda r, t: send_g(r, t, gmix, down))

    weights_sent()


def widen(
    so_in, ig_in, gw_in, small, so, ig, gain, bias, w_in, b_in, w_out, b_out, so_b, ig_b, gw_b, ig_f, w1_f, w2_f, s_in, s_out
):
    n_rows = ig_b.shape[0]
    width, half = w1_f.shape
    part = half // 4
    loads = []
    for i in range(8):
        rows = pl.ds((i // 2) * part, part)
        loads.append(pltpu.make_async_copy(gw_in.at[i % 2, rows], gw_b.at[i % 2, rows], s_in.at[i]))
    for r in range(n_rows):
        loads.append(pltpu.make_async_copy(ig_in.at[r], ig_b.at[r], s_in.at[9 + r]))
    loads.append(pltpu.make_async_copy(so_in, so_b, s_in.at[8]))
    for load in loads:
        load.start()
    width_half = width // 2
    gain[...] = small[0:1, 0:width]
    bias[...] = small[1:2, 0:width]
    b_in[...] = small[2:3, :]
    b_out[...] = small[3:4, 0:width_half]
    stores = []
    for i in range(4):
        rows = pl.ds(i * part, part)
        loads[2 * i].wait()
        w1_f[:, rows] = gw_b[0, rows].T.astype(F32)
        stores.append(pltpu.make_async_copy(w1_f.at[:, rows], w_in.at[0, :, rows], s_out.at[1 + 2 * i]))
        stores[-1].start()
        loads[2 * i + 1].wait()
        w2_f[rows] = gw_b[1, rows].astype(F32)
        stores.append(pltpu.make_async_copy(w2_f.at[rows], w_out.at[0, rows], s_out.at[2 + 2 * i]))
        stores[-1].start()
    for r in range(n_rows):
        loads[8 + r].wait()
        ig_f[r] = ig_b[r].astype(F32)
        stores.append(pltpu.make_async_copy(ig_f.at[r], ig.at[0, r], s_out.at[9 + r]))
        stores[-1].start()
    loads[-1].wait()
    stores.append(pltpu.make_async_copy(so_b, so.at[0], s_out.at[0]))
    stores[-1].start()
    for store in stores:
        store.wait()


def per_device(block_input, out_cotangent, lengths, ln_gain, ln_bias, w_in, b_in, w_out, b_out):
    n_rows, seq, width = block_input.shape
    half = w_in.shape[2]
    dp_count = lax.axis_size("dp")
    levels = int(math.log2(dp_count)) - 1
    chunks = seq // CHUNK
    quarter = half // 4
    cos_w, sin_w = dft_pair(width)
    cos_s, sin_s = dft_pair(seq)
    wt = jnp.asarray(np.concatenate([cos_w, sin_w], axis=1).astype(ml_dtypes.bfloat16))
    st = jnp.asarray(np.concatenate([cos_s, -sin_s], axis=1).astype(ml_dtypes.bfloat16))
    row_block = (n_rows, seq, width)
    dma = pltpu.SemaphoreType.DMA
    vmem = pl.BlockSpec(memory_space=pltpu.VMEM)
    anywhere = pl.BlockSpec(memory_space=pl.ANY)
    by_chunk = [dma((n_rows, chunks))] * 8
    scratch = [
        pltpu.VMEM((width, half), BF16),
        pltpu.VMEM((half, width), BF16),
        pltpu.VMEM((width, half), BF16),
        pltpu.VMEM((half, width), BF16),
        pltpu.VMEM((width, 2 * width), BF16),
        pltpu.VMEM((seq, 2 * seq), BF16),
        *[pltpu.VMEM(row_block, BF16) for _ in range(9)],
        pltpu.VMEM((n_rows, seq, half), BF16),
        pltpu.VMEM((n_rows, seq, half), BF16),
        pltpu.VMEM((1, seq, half), BF16),
        pltpu.VMEM((n_rows, seq, half), BF16),
        pltpu.VMEM((seq, 2 * width), BF16),
        pltpu.VMEM((seq, width), BF16),
        pltpu.VMEM(row_block, F32),
        pltpu.VMEM(row_block, F32),
        pltpu.VMEM((n_rows, seq, 1), F32),
        pltpu.VMEM((n_rows, seq, 1), F32),
        pltpu.VMEM((2, 8, half), F32),
        pltpu.VMEM((2, half, width), BF16),
        pltpu.VMEM((half, width), BF16),
        pltpu.VMEM((2, quarter, width), BF16),
        pltpu.VMEM((levels - 1, quarter, width), BF16),
        pltpu.VMEM((levels + 1, 8, half), F32),
        pltpu.VMEM((levels + 1, 8, half), F32),
        pltpu.VMEM((8, half), F32),
        pltpu.SemaphoreType.REGULAR,
        dma((6,)),
        dma((3,)),
        dma,
        dma,
        *by_chunk,
        *[dma((4,))] * 6,
        dma((4,)),
        dma((4,)),
        dma((4,)),
        dma((4,)),
        dma((2,)),
        dma((2,)),
        dma((levels - 1,)),
        dma((levels - 1,)),
        dma((7 + levels,)),
        dma((7 + levels,)),
        dma((4,)),
        dma((4,)),
        dma((3,)),
        dma((3,)),
        dma((levels + 1,)),
        dma((levels + 1,)),
    ]
    section_out, input_grad, weight_grad, small = pl.pallas_call(
        functools.partial(relay, dp_count),
        out_shape=(
            jax.ShapeDtypeStruct(row_block, BF16),
            jax.ShapeDtypeStruct(row_block, BF16),
            jax.ShapeDtypeStruct((2, half, width), BF16),
            jax.ShapeDtypeStruct((8, half), F32),
        ),
        in_specs=[
            pl.BlockSpec(memory_space=pltpu.SMEM),
            anywhere,
            anywhere,
            vmem,
            vmem,
            vmem,
            vmem,
            anywhere,
            anywhere,
            anywhere,
            anywhere,
        ],
        out_specs=(anywhere, anywhere, anywhere, vmem),
        scratch_shapes=scratch,
        compiler_params=pltpu.CompilerParams(
            collective_id=0, has_side_effects=True, vmem_limit_bytes=62 * 2**20
        ),
        name="fnet_relay",
    )(lengths, block_input, out_cotangent, ln_gain, ln_bias, b_in, b_out, w_in[0], w_out[0], wt, st)
    return pl.pallas_call(
        widen,
        out_shape=(
            jax.ShapeDtypeStruct((1, *row_block), BF16),
            jax.ShapeDtypeStruct((1, *row_block), F32),
            jax.ShapeDtypeStruct((1, width), F32),
            jax.ShapeDtypeStruct((1, width), F32),
            jax.ShapeDtypeStruct((1, width, half), F32),
            jax.ShapeDtypeStruct((1, half), F32),
            jax.ShapeDtypeStruct((1, half, width), F32),
            jax.ShapeDtypeStruct((1, width // 2), F32),
        ),
        in_specs=[anywhere, anywhere, anywhere, vmem],
        out_specs=(anywhere, anywhere, vmem, vmem, anywhere, vmem, anywhere, vmem),
        scratch_shapes=[
            pltpu.VMEM(row_block, BF16),
            pltpu.VMEM(row_block, BF16),
            pltpu.VMEM((2, half, width), BF16),
            pltpu.VMEM(row_block, F32),
            pltpu.VMEM((width, half), F32),
            pltpu.VMEM((half, width), F32),
            dma((9 + n_rows,)),
            dma((9 + n_rows,)),
        ],
        compiler_params=pltpu.CompilerParams(vmem_limit_bytes=62 * 2**20),
        name="widen",
    )(section_out, input_grad, weight_grad, small)


def solution(mesh):
    in_specs = (
        P("dp", None, None),
        P("dp", None, None),
        P("dp"),
        P("section", None),
        P("section", None),
        P("section", None, None),
        P("section", None),
        P("section", None, None),
        P("section", None),
    )
    out_specs = (
        P("section", "dp", None, None),
        P("section", "dp", None, None),
        P("section", None),
        P("section", None),
        P("section", None, None),
        P("section", None),
        P("section", None, None),
        P("section", None),
    )
    return jax.shard_map(
        per_device, mesh=mesh, in_specs=in_specs, out_specs=out_specs, check_vma=False
    )
```

time: 209 us -> 156 us (0.75)
  Pallas kernels: 188 us -> 155 us
  local copies, waits for them, and re-layouts: 11.5 us -> 0 us
  other arithmetic: 8.73 us -> 0 us
    pallas_call x1, Pallas kernels: 188 us -> 147 us  [per_device(): pl.pallas_call(functools.partial(relay, dp_count), out_shape=(jax.ShapeDt...]
    pallas_call x0 -> x1, Pallas kernels: none -> 8.54 us  [per_device(): pl.pallas_call(widen, out_shape=(jax.ShapeDtypeStruct((1, *row_block), BF...]
    unnamed x6 -> x0, local copies, waits for them, and re-layouts: 7.36 us -> none
    convert_element_type x1 -> x0, other arithmetic: 6.83 us -> none  [per_device(): weight_grad[1].astype(F32)[None]]
    slice x2 -> x0, local copies, waits for them, and re-layouts: 2.8 us -> none  [the longest x1 1.4 us: per_device(): small[1:2, 0:width]]
where the time goes in v2:
time: 156 us
  Pallas kernels  155 us (99%)
    pallas_call x1, Pallas kernels, per_device(): pl.pallas_call(functools.partial(relay, dp_count), out_shape=(jax.ShapeDt...  147 us
    pallas_call x1, Pallas kernels, per_device(): pl.pallas_call(widen, out_shape=(jax.ShapeDtypeStruct((1, *row_block), BF...  8.54 us

profile of v2, /device:TPU:0, one launch (start us, length us, event | category | flops | bytes accessed | tf_op | source)
XLA Modules:
  0.0 156.0 jit_solution(14923950409271665171)
XLA Ops:
  0.6 146.7 %fnet_relay.1 = (bf16[2,512,768]{2,1,0:T(8,128)(2,1)}, bf16[2,512,768]{2,1,0:T(8,128)(2,1)}, bf16[2,1536,768]{2,1,0:T(8,128)(2,1)}, f32[8,1536]{1,0:T(8,128)}) custom-call(s32[2]{0:T(128)} %lengths.1, bf16[2,512,768]{2,1,0:T(8,128)(2,1)} %x_hbm.1, bf16[2,512,768]{2,1,0:T(8,128)(2,1)} %cot_hbm.1, f32[1,768]{1,0:T(1,128)} %gain_ref.1, f32[1,768]{1,0:T(1,128)} %bias_ref.1, ...), custom_call_target="tpu_custom_call" | custom-call | tf_op jit(solution)/shard_map/fnet_relay/pallas_call | solution.py:894
  147.3 8.5 %widen.1 = (bf16[1,2,512,768]{3,2,1,0:T(8,128)(2,1)}, f32[1,2,512,768]{3,2,1,0:T(8,128)}, f32[1,768]{1,0:T(1,128)}, f32[1,768]{1,0:T(1,128)}, f32[1,768,1536]{2,...) custom-call(bf16[2,512,768]{2,1,0:T(8,128)(2,1)} %get-tuple-element.12.so_in, ...), custom_call_target="tpu_custom_call" | custom-call | tf_op jit(solution)/shard_map/widen/pallas_call | solution.py:922

commit v3 on v2

--- a/solution.py
+++ b/solution.py
@@ -266,6 +266,7 @@
         for j in range(2 * width // 512):
             cols = pl.ds(j * 512, 512)
             sp[:, cols] = dot(hin[r], wt[:, cols]).astype(BF16)
+        pl.when(r == 0)(swap_par.wait)
         for t in range(chunks):
             rows = rows_of(t)
             z = (
@@ -491,7 +492,6 @@
     load_st.wait()
     load_w1.wait()
     load_w2.wait()
-    swap_par.wait()
 
     @pl.when(first_layer)
     def _():
@@ -702,13 +702,14 @@
 
             grads()
 
-        late = first_layer & last
-        pl.when((backward & jnp.logical_not(first_layer & (r == n_rows - 1))) | late)(
+        put_off = first_layer & (core == 1)
+        late = put_off & last
+        in_turn = backward & jnp.logical_not(put_off & (r == n_rows - 1))
+        pl.when(in_turn | late)(
             lambda: part_back(jnp.where(late, n_rows - 1, r))
         )
 
         now = jnp.where(late, n_rows - 1, r)
-        in_turn = backward & jnp.logical_not(first_layer & (r == n_rows - 1))
         pl.when(((section == 2) & in_turn) | ((section == 0) & (in_turn | late)))(lambda: mix_backward(now, gout))
         return carry
 

time: 156 us -> 156 us (level)
  no operation moved by 1% of the time
where the time goes in v3:
time: 156 us
  Pallas kernels  155 us (99%)
    pallas_call x1, Pallas kernels, per_device(): pl.pallas_call(functools.partial(relay, dp_count), out_shape=(jax.ShapeDt...  147 us
    pallas_call x1, Pallas kernels, per_device(): pl.pallas_call(widen, out_shape=(jax.ShapeDtypeStruct((1, *row_block), BF...  8.54 us

profile of v3, /device:TPU:0, one launch (start us, length us, event | category | flops | bytes accessed | tf_op | source)
XLA Modules:
  0.0 155.9 jit_solution(7117465720825274140)
XLA Ops:
  0.6 146.6 %fnet_relay.1 = (bf16[2,512,768]{2,1,0:T(8,128)(2,1)}, bf16[2,512,768]{2,1,0:T(8,128)(2,1)}, bf16[2,1536,768]{2,1,0:T(8,128)(2,1)}, f32[8,1536]{1,0:T(8,128)}) custom-call(s32[2]{0:T(128)} %lengths.1, bf16[2,512,768]{2,1,0:T(8,128)(2,1)} %x_hbm.1, bf16[2,512,768]{2,1,0:T(8,128)(2,1)} %cot_hbm.1, f32[1,768]{1,0:T(1,128)} %gain_ref.1, f32[1,768]{1,0:T(1,128)} %bias_ref.1, ...), custom_call_target="tpu_custom_call" | custom-call | tf_op jit(solution)/shard_map/fnet_relay/pallas_call | solution.py:895
  147.2 8.5 %widen.1 = (bf16[1,2,512,768]{3,2,1,0:T(8,128)(2,1)}, f32[1,2,512,768]{3,2,1,0:T(8,128)}, f32[1,768]{1,0:T(1,128)}, f32[1,768]{1,0:T(1,128)}, f32[1,768,1536]{2,...) custom-call(bf16[2,512,768]{2,1,0:T(8,128)(2,1)} %get-tuple-element.12.so_in, ...), custom_call_target="tpu_custom_call" | custom-call | tf_op jit(solution)/shard_map/widen/pallas_call | solution.py:923
